TPU v7x, 32 devices: a whole 2x2x4 slice. The times are simulated.
32 devices in a mesh: pp: 4 (over y, core), node: 2 (over x), local: 4 (over z).
Axes of the slice: x: 2, y: 2, z: 4, core: 2. Of those that a mesh axis runs over, the one named last changes fastest.
Arguments:
- act_fwd: bfloat16 [4, 1024, 4096], P('pp', ('node', 'local')), may hold values from -6 to 6
- routes_fwd: int32 [4, 1024, 1], P('pp', ('node', 'local')), may hold values from 0 to 1; in each aligned block of 128 rows (0 to 127, 128 to 255, ..., all dimensions but the last counted through in order) at most 80 rows name the same one
- weight_fwd: float32 [4, 1024], P('pp', ('node', 'local')), may hold values from 0.25 to 1
- grad_bwd: bfloat16 [4, 1024, 4096], P('pp', ('node', 'local')), may hold values from -6 to 6
- routes_bwd: int32 [4, 1024, 1], P('pp', ('node', 'local')), may hold values from 0 to 1; in each aligned block of 128 rows (0 to 127, 128 to 255, ..., all dimensions but the last counted through in order) at most 80 rows name the same one
- weight_bwd: float32 [4, 1024], P('pp', ('node', 'local')), may hold values from 0.25 to 1
- saved_bwd: bfloat16 [4, 1024, 2048], P('pp', ('node', 'local')), may hold values from -8 to 8
- w_gate_up: bfloat16 [4, 2, 4096, 2048], P('pp', 'node', 'local'), may hold values from -0.09375 to 0.09375
- w_down: bfloat16 [4, 2, 1024, 4096], P('pp', 'node', None, 'local'), may hold values from -0.1875 to 0.1875
Outputs:
- next_input: bfloat16 [4, 1024, 4096], P('pp', ('node', 'local'))
- prev_grad: bfloat16 [4, 1024, 4096], P('pp', ('node', 'local'))
Inputs may be any that keep to these rules, and one draw needn't show every extreme that they name: `routes_fwd`: within each device's 128 tokens (aligned blocks of rows), no expert is named more than 80 times, a bound that some block reaches. `routes_bwd`: within each device's 128 tokens (aligned blocks of rows), no expert is named more than 80 times, a bound that some block reaches.
All inputs are finite; a program needn't handle non-finite values.
Results may differ from a plain program's by a relative error of at most 0.017.
Values may be sent and summed in bfloat16 or wider, within the bound.
No kernel may reach another device: no remote copies, remote signals or barrier semaphores. Data moves between devices by JAX's collectives and lax.ppermute only.
A program may use at most 128 MiB of HBM per device.

v0:
```python
import jax
import jax.numpy as jnp
from jax import lax
from jax.sharding import PartitionSpec as P

F32 = jnp.float32
BF16 = jnp.bfloat16
AXES = ("pp", "node", "local")


def move(value, by_pp=0, by_node=0, by_local=0, wrap=True, first=0, last=None):
    pps, nodes, locs = (lax.axis_size(a) for a in AXES)
    last = locs - 1 if last is None else last
    pairs = []
    for s in range(pps):
        for n in range(nodes):
            for l in range(locs):
                to = l + by_local
                if not wrap and not (first <= l <= last and 0 <= to < locs):
                    continue
                source = (s * nodes + n) * locs + l
                target = (((s + by_pp) % pps) * nodes + (n ^ by_node)) * locs + to % locs
                pairs.append((source, target))
    return lax.ppermute(value, AXES, pairs)


def sorted_places(route):
    ones = route.astype(F32)
    count = route.shape[0]
    earlier = (jnp.arange(count)[None, :] < jnp.arange(count)[:, None]).astype(F32)
    ones_before = jnp.dot(earlier, ones[:, None], preferred_element_type=F32)[:, 0]
    zeros = count - jnp.sum(ones)
    index = jnp.arange(count, dtype=F32)
    place = jnp.where(route == 0, index - ones_before, zeros + ones_before)
    return place.astype(jnp.int32)


def sorter(route):
    place = sorted_places(route)
    rows = jnp.arange(route.shape[0], dtype=jnp.int32)
    return (rows[:, None] == place[None, :]).astype(BF16)


def window_placer(route, node, capacity):
    place = sorted_places(route)
    start = route.shape[0] - capacity
    in_window = place - jnp.where(route == 1, start, 0)
    row = jnp.where(route == node, in_window, in_window + capacity)
    rows = jnp.arange(2 * capacity, dtype=jnp.int32)
    return (rows[:, None] == row[None, :]).astype(BF16)


def dot_t(left, right):
    return lax.dot_general(left, right, (((1,), (1,)), ((), ())), preferred_element_type=F32)


def windows(blocks, node, capacity):
    tokens = blocks.shape[-2]
    start = tokens - capacity
    low = lax.slice_in_dim(blocks, 0, capacity, axis=-2 + blocks.ndim)
    high = lax.slice_in_dim(blocks, start, tokens, axis=-2 + blocks.ndim)
    own = jnp.where(node == 0, low, high)
    other = jnp.where(node == 0, high, low)
    return own, other


def join(*values):
    return lax.optimization_barrier(values)


def to_owners(tokens, placer, local, after=()):
    column = tokens.shape[1] // 4
    blocks = []
    for m in range(4):
        block = lax.dynamic_slice_in_dim(tokens, ((local - m) % 4) * column, column, axis=1)
        blocks.append(jnp.dot(placer, block, preferred_element_type=F32).astype(BF16))
    if after:
        blocks = join(*blocks, *after)[:4]
    return join(blocks[0], *(move(blocks[m], by_local=-m) for m in (1, 2, 3)))


def to_expert(blocks, node, capacity):
    own, other = windows(jnp.stack(blocks), node, capacity)
    got = move(other, by_node=1)
    return jnp.stack([own, got], axis=1)


def reduce_scatter(partial):
    right, left = partial[3], partial[1]
    for step in (1, 2, 3):
        got_r = move(right.astype(BF16), by_local=1, wrap=False, last=step - 1)
        got_l = move(left.astype(BF16), by_local=-1, wrap=False, first=4 - step)
        right = partial[3 - step] + got_r.astype(F32)
        if step < 3:
            left = partial[step + 1] + got_l.astype(F32)
    return right + got_l.astype(F32)


def all_gather(rows, local):
    from_left, from_right = [rows], [rows]
    for step in (1, 2, 3):
        from_left.append(move(from_left[-1], by_local=1, wrap=False, first=step - 1))
        from_right.append(move(from_right[-1], by_local=-1, wrap=False, last=4 - step))
    slots = [rows]
    for m in (1, 2, 3):
        slots.append(jnp.where(local + m < 4, from_right[m], from_left[4 - m]))
    return jnp.stack(slots)


def give_back(done, by_pp):
    got = []
    for m in (2, 1, 3, 0):
        got.append(move(done[m, 0], by_pp=by_pp, by_local=m))
        got.append(move(done[m, 1], by_pp=by_pp, by_node=1, by_local=m))
    got = join(*got)
    rows = [None] * 4
    for i, m in enumerate((2, 1, 3, 0)):
        rows[m] = jnp.concatenate([got[2 * i], got[2 * i + 1]], axis=0)
    return rows


def unsort(blocks, placer, local):
    column = blocks[0].shape[1]
    full = jnp.zeros((placer.shape[1], 4 * column), F32)
    for m in range(4):
        moe = lax.dot_general(
            placer, blocks[m], (((0,), (0,)), ((), ())), preferred_element_type=F32
        )
        full = lax.dynamic_update_slice_in_dim(full, moe, ((local - m) % 4) * column, axis=1)
    return full


def body_pair(
    act_fwd, routes_fwd, weight_fwd, grad_bwd, routes_bwd, weight_bwd, saved_bwd, w_gate_up, w_down
):
    node = lax.axis_index("node")
    local = lax.axis_index("local")
    tokens_here = act_fwd.shape[1]
    capacity = 5 * tokens_here // 8
    w_gu = w_gate_up[0, 0]
    w_dn = w_down[0, 0]
    hidden_units = w_dn.shape[0]

    act = act_fwd[0]
    grad = grad_bwd[0]
    sort_a = sorter(routes_fwd[0, :, 0])
    sort_b = sorter(routes_bwd[0, :, 0])
    dy = (weight_bwd[0][:, None] * grad.astype(F32)).astype(BF16)
    blocks_b = to_owners(dy, sort_b, local)
    blocks_a = to_owners(act, sort_a, local, after=blocks_b[1:])
    rows_b = to_expert(blocks_b, node, capacity)
    rows_a = to_expert(blocks_a, node, capacity)
    saved = jnp.dot(sort_b, saved_bwd[0], preferred_element_type=F32).astype(BF16)
    saved_own, saved_other = windows(saved, node, capacity)
    saved_rows = jnp.stack([saved_own, move(saved_other, by_node=1)])

    act_next = move(act, by_pp=1)
    grad_next = move(grad, by_pp=-1)
    route_a_next = move(routes_fwd[0, :, 0], by_pp=1)
    route_b_next = move(routes_bwd[0, :, 0], by_pp=-1)
    weight_next = move(weight_fwd[0], by_pp=1)

    shape = (4, 2, capacity)
    column = rows_a.shape[-1]
    part_a = jnp.dot(rows_a.reshape(-1, column), w_gu, preferred_element_type=F32)
    preact = reduce_scatter(part_a.reshape(shape + (2 * hidden_units,)))
    part_b = dot_t(rows_b.reshape(-1, column), w_dn)
    dh = reduce_scatter(part_b.reshape(shape + (hidden_units,)))

    hidden = (jax.nn.silu(preact[..., :hidden_units]) * preact[..., hidden_units:]).astype(BF16)
    all_hidden = all_gather(hidden, local)
    done_a = jnp.dot(
        all_hidden.reshape(-1, hidden_units), w_dn, preferred_element_type=F32
    ).astype(BF16)

    g = saved_rows[..., :hidden_units].astype(F32)
    u = saved_rows[..., hidden_units:].astype(F32)
    q = 1.0 / (1.0 + jnp.exp(-g))
    grad_gu = jnp.concatenate([dh * u * q * (1.0 + g * (1.0 - q)), dh * g * q], axis=-1).astype(
        BF16
    )
    all_gu = all_gather(grad_gu, local)
    done_b = dot_t(all_gu.reshape(-1, 2 * hidden_units), w_gu).astype(BF16)

    back_a = give_back(done_a.reshape(shape + (column,)), 1)
    back_b = give_back(done_b.reshape(shape + (column,)), -1)

    moe_a = unsort(back_a, window_placer(route_a_next, node, capacity), local)
    next_input = (act_next.astype(F32) + weight_next[:, None] * moe_a).astype(BF16)
    moe_b = unsort(back_b, window_placer(route_b_next, node, capacity), local)
    prev_grad = (grad_next.astype(F32) + moe_b).astype(BF16)
    return next_input[None], prev_grad[None]


def from_behind(value, axis, by):
    length = lax.axis_size(axis)
    return lax.ppermute(value, axis, [(i, (i + by) % length) for i in range(length)])


def place_matrix(route, expert_count, capacity):
    onehot = (route[:, None] == jnp.arange(expert_count, dtype=jnp.int32)[None, :]).astype(
        jnp.int32
    )
    before = jnp.cumsum(onehot, axis=0) - onehot
    slot_index = jnp.sum(before * onehot, axis=1)
    target = route * capacity + slot_index
    positions = jnp.arange(expert_count * capacity, dtype=jnp.int32)
    return (positions[:, None] == target[None, :]).astype(jnp.bfloat16)


def pack_rows(placer, values, expert_count, capacity):
    packed = jnp.dot(placer, values, preferred_element_type=jnp.float32).astype(jnp.bfloat16)
    return packed.reshape(expert_count, capacity, values.shape[1])


def unpack_rows(placer, packed):
    flattened = packed.reshape(-1, packed.shape[-1])
    result = lax.dot_general(
        placer, flattened, (((0,), (0,)), ((), ())), preferred_element_type=jnp.float32
    )
    return result.astype(jnp.bfloat16)


def flat_outgoing(packed, local_count):
    expert_count, capacity, feature_count = packed.shape
    column = feature_count // local_count
    outgoing = packed.reshape(expert_count, capacity, local_count, column).transpose(0, 2, 1, 3)
    return outgoing.reshape(expert_count * local_count, capacity, column)


def flat_layout(received, expert_count, local_count):
    capacity = received.shape[1]
    column = received.shape[2]
    rows_in = received.reshape(expert_count, local_count, capacity, column).transpose(1, 0, 2, 3)
    return rows_in.reshape(-1, column)


def send_rows(packs, local_count):
    expert_count = packs[0].shape[0]
    outgoing = tuple((flat_outgoing(packed, local_count) for packed in packs))
    received = (
        lax.all_to_all(outgoing[0], ("node", "local"), split_axis=0, concat_axis=0, tiled=True),
        lax.all_to_all(outgoing[1], ("node", "local"), split_axis=0, concat_axis=0, tiled=True),
    )
    return tuple((flat_layout(item, expert_count, local_count) for item in received))


def return_rows(finished_pair, expert_count, capacity, local_count):
    column = finished_pair[0].shape[1]
    blocks = tuple(
        (item.reshape(local_count, expert_count, capacity, column) for item in finished_pair)
    )
    outgoing = tuple(
        (
            item.transpose(1, 0, 2, 3).reshape(expert_count * local_count, capacity, column)
            for item in blocks
        )
    )
    received = (
        lax.all_to_all(outgoing[0], ("node", "local"), split_axis=0, concat_axis=0, tiled=True),
        lax.all_to_all(outgoing[1], ("node", "local"), split_axis=0, concat_axis=0, tiled=True),
    )
    results = []
    for item in received:
        arranged = item.reshape(expert_count, local_count, capacity, column).transpose(0, 2, 1, 3)
        results.append(arranged.reshape(expert_count, capacity, local_count * column))
    return tuple(results)


def body(
    act_fwd, routes_fwd, weight_fwd, grad_bwd, routes_bwd, weight_bwd, saved_bwd, w_gate_up, w_down
):
    node_count = lax.axis_size("node")
    local_count = lax.axis_size("local")
    tokens_here = act_fwd.shape[1]
    capacity = 5 * tokens_here // (4 * node_count)
    rows_each = node_count * capacity
    w_gu = w_gate_up[0, 0]
    w_dn = w_down[0, 0]
    hidden_units = w_dn.shape[0]
    tokens_a = act_fwd[0]
    placer_a = place_matrix(routes_fwd[0, :, 0], node_count, capacity)
    cotangent = grad_bwd[0]
    placer_b = place_matrix(routes_bwd[0, :, 0], node_count, capacity)
    scaled = (weight_bwd[0][:, None] * cotangent.astype(jnp.float32)).astype(jnp.bfloat16)
    packed_a = pack_rows(placer_a, tokens_a, node_count, capacity)
    packed_b = pack_rows(placer_b, scaled, node_count, capacity)
    rows_a, rows_b = send_rows((packed_a, packed_b), local_count)
    saved_packed = pack_rows(placer_b, saved_bwd[0], node_count, capacity)
    saved_rows = lax.all_to_all(
        saved_packed, "node", split_axis=0, concat_axis=0, tiled=True
    ).reshape(rows_each, -1)
    row_block = rows_a
    preact = lax.psum_scatter(
        jnp.dot(row_block, w_gu, preferred_element_type=jnp.float32).astype(jnp.bfloat16),
        "local",
        scatter_dimension=0,
        tiled=True,
    ).astype(jnp.float32)
    row_block = rows_b
    grad_hidden = lax.psum_scatter(
        lax.dot_general(
            row_block, w_dn, (((1,), (1,)), ((), ())), preferred_element_type=jnp.float32
        ).astype(jnp.bfloat16),
        "local",
        scatter_dimension=0,
        tiled=True,
    ).astype(jnp.float32)
    hidden = (jax.nn.silu(preact[:, :hidden_units]) * preact[:, hidden_units:]).astype(jnp.bfloat16)
    done_a = jnp.dot(
        lax.all_gather(hidden, "local", axis=0, tiled=True),
        w_dn,
        preferred_element_type=jnp.float32,
    ).astype(jnp.bfloat16)
    gate_pre = saved_rows[:, :hidden_units].astype(jnp.float32)
    up_pre = saved_rows[:, hidden_units:].astype(jnp.float32)
    sigmoid_g = 1.0 / (1.0 + jnp.exp(-gate_pre))
    grad_gate = grad_hidden * up_pre * sigmoid_g * (1.0 + gate_pre * (1.0 - sigmoid_g))
    grad_up = grad_hidden * gate_pre * sigmoid_g
    grad_gu = jnp.concatenate([grad_gate, grad_up], axis=1).astype(jnp.bfloat16)
    product = lax.dot_general(
        lax.all_gather(grad_gu, "local", axis=0, tiled=True),
        w_gu,
        (((1,), (1,)), ((), ())),
        preferred_element_type=jnp.float32,
    )
    done_b = product.astype(jnp.bfloat16)
    back_a, back_b = return_rows((done_a, done_b), node_count, capacity, local_count)
    moe_a = unpack_rows(placer_a, back_a)
    result_a = tokens_a.astype(jnp.float32) + weight_fwd[0][:, None] * moe_a.astype(jnp.float32)
    result_a = result_a.astype(jnp.bfloat16)
    moe_b = unpack_rows(placer_b, back_b)
    result_b = (cotangent.astype(jnp.float32) + moe_b.astype(jnp.float32)).astype(jnp.bfloat16)
    next_input = from_behind(result_a[None], "pp", 1)
    prev_grad = from_behind(result_b[None], "pp", -1)
    return (next_input, prev_grad)


def solution(mesh):
    in_specs = (
        P("pp", ("node", "local"), None),
        P("pp", ("node", "local"), None),
        P("pp", ("node", "local")),
        P("pp", ("node", "local"), None),
        P("pp", ("node", "local"), None),
        P("pp", ("node", "local")),
        P("pp", ("node", "local"), None),
        P("pp", "node", "local", None),
        P("pp", "node", None, "local"),
    )
    out_specs = (P("pp", ("node", "local"), None), P("pp", ("node", "local"), None))
    paired = mesh.shape["node"] == 2 and mesh.shape["local"] == 4
    plan = body_pair if paired else body
    return jax.shard_map(plan, mesh=mesh, in_specs=in_specs, out_specs=out_specs, check_vma=False)
```

profile of v0, /device:TPU:0, one launch (start us, length us, event | category | flops | bytes accessed | tf_op | source)
XLA Modules:
  0.0 297.0 jit_solution(5903647847098998153)
XLA Ops:
  6.1 5.1 %collective-permute-start.3 = (bf16[128,1024]{1,0:T(8,128)(2,1)}, bf16[128,1024]{1,0:T(8,128)(2,1)}, u32[]{:S(2)}, u32[]{:S(2)}) collective-permute-start(bf16[128,1024]{1,0:T(8,128)(2,1)} %convolution_convert_fusion.3), channel_id=1, source_target_pairs={{0,3},{1,0},{2,1},{3,2},{4,7},{5,4},{6,5},{7,6},{8,11},{9,8},{10,9... | collective-permute-start | bytes 786440 | tf_op jit(solution)/shard_map/ppermute | solution.py:24
  22.5 11.3 %collective-permute-done.4 = bf16[128,1024]{1,0:T(8,128)(2,1)} collective-permute-done((bf16[128,1024]{1,0:T(8,128)(2,1)}, bf16[128,1024]{1,0:T(8,128)(2,1)}, u32[]{:S(2)}, u32[]{:S(2)}) %collective-permute-start.4) | collective-permute-done | bytes 262176 | tf_op jit(solution)/shard_map/ppermute | solution.py:24
  33.8 9.1 %collective-permute-start.7 = (bf16[128,1024]{1,0:T(8,128)(2,1)}, bf16[128,1024]{1,0:T(8,128)(2,1)S(1)}, u32[]{:S(2)}, u32[]{:S(2)}) collective-permute-start(bf16[128,1024]{1,0:T(8,128)(2,1)} %convolution_convert_fusion.6), channel_id=1, source_target_pairs={{0,2},{1,3},{2,0},{3,1},{4,6},{5,7},{6,4},{7,5},{8,10},{9,11},{10,... | collective-permute-start | bytes 786440 | tf_op jit(solution)/shard_map/ppermute | solution.py:24
  48.2 18.2 %collective-permute-done.7 = bf16[128,1024]{1,0:T(8,128)(2,1)S(1)} collective-permute-done((bf16[128,1024]{1,0:T(8,128)(2,1)}, bf16[128,1024]{1,0:T(8,128)(2,1)S(1)}, u32[]{:S(2)}, u32[]{:S(2)}) %collective-permute-start.7) | collective-permute-done | bytes 262176 | tf_op jit(solution)/shard_map/ppermute | solution.py:24
  73.3 9.6 %collective-permute-done.9 = bf16[4,80,1024]{2,1,0:T(8,128)(2,1)S(1)} collective-permute-done((bf16[4,80,1024]{2,1,0:T(8,128)(2,1)S(1)}, bf16[4,80,1024]{2,1,0:T(8,128)(2,1)S(1)}, u32[]{:S(2)}, u32[]{:S(2)}) %collective-permute-start.9) | collective-permute-done | bytes 655392 | tf_op jit(solution)/shard_map/ppermute | solution.py:24
  85.1 2.9 fusion.2
  96.5 14.6 %collective-permute-done.34 = bf16[2,80,1024]{2,1,0:T(8,128)(2,1)S(1)} collective-permute-done((bf16[2,80,1024]{2,1,0:T(8,128)(2,1)S(1)}, bf16[2,80,1024]{2,1,0:T(8,128)(2,1)S(1)}, u32[]{:S(2)}, u32[]{:S(2)}) %collective-permute-start.34) | collective-permute-done | bytes 327712 | tf_op jit(solution)/shard_map/ppermute | solution.py:24
  111.8 5.1 %collective-permute-start.35 = (bf16[2,80,1024]{2,1,0:T(8,128)(2,1)}, bf16[2,80,1024]{2,1,0:T(8,128)(2,1)}, u32[]{:S(2)}, u32[]{:S(2)}) collective-permute-start(bf16[2,80,1024]{2,1,0:T(8,128)(2,1)} %add_convert_fusion.8), channel_id=1, source_target_pairs={{0,1},{1,2},{2,3},{4,5},{5,6},{6,7},{8,9},{9,10},{10,11},{12,13},{... | collective-permute-start | bytes 983048 | tf_op jit(solution)/shard_map/ppermute | solution.py:24
  120.6 5.4 %collective-permute-start.11 = (bf16[2,80,2048]{2,1,0:T(8,128)(2,1)}, bf16[2,80,2048]{2,1,0:T(8,128)(2,1)}, u32[]{:S(2)}, u32[]{:S(2)}) collective-permute-start(bf16[2,80,2048]{2,1,0:T(8,128)(2,1)} %get-tuple-element.84), channel_id=1, source_target_pairs={{0,1},{1,2},{4,5},{5,6},{8,9},{9,10},{12,13},{13,14},{16,17},{17,1... | collective-permute-start | bytes 1966088 | tf_op jit(solution)/shard_map/ppermute | solution.py:24
  130.9 2.4 collective-permute-start.41
  133.4 6.4 %collective-permute-done.11 = bf16[2,80,2048]{2,1,0:T(8,128)(2,1)} collective-permute-done((bf16[2,80,2048]{2,1,0:T(8,128)(2,1)}, bf16[2,80,2048]{2,1,0:T(8,128)(2,1)}, u32[]{:S(2)}, u32[]{:S(2)}) %collective-permute-start.11) | collective-permute-done | bytes 655392 | tf_op jit(solution)/shard_map/ppermute | solution.py:24
  143.1 5.0 %collective-permute-start.12 = (bf16[2,80,2048]{2,1,0:T(8,128)(2,1)}, bf16[2,80,2048]{2,1,0:T(8,128)(2,1)S(1)}, u32[]{:S(2)}, u32[]{:S(2)}) collective-permute-start(bf16[2,80,2048]{2,1,0:T(8,128)(2,1)} %add_convert_fusion.4), channel_id=1, source_target_pairs={{0,1},{1,2},{2,3},{4,5},{5,6},{6,7},{8,9},{9,10},{10,11},{12,13},{... | collective-permute-start | bytes 1966088 | tf_op jit(solution)/shard_map/ppermute | solution.py:24
  156.0 9.1 %collective-permute-done.12 = bf16[2,80,2048]{2,1,0:T(8,128)(2,1)S(1)} collective-permute-done((bf16[2,80,2048]{2,1,0:T(8,128)(2,1)}, bf16[2,80,2048]{2,1,0:T(8,128)(2,1)S(1)}, u32[]{:S(2)}, u32[]{:S(2)}) %collective-permute-start.12) | collective-permute-done | bytes 655392 | tf_op jit(solution)/shard_map/ppermute | solution.py:24
  165.1 3.1 %collective-permute-done.15 = bf16[2,80,2048]{2,1,0:T(8,128)(2,1)} collective-permute-done((bf16[2,80,2048]{2,1,0:T(8,128)(2,1)S(1)}, bf16[2,80,2048]{2,1,0:T(8,128)(2,1)}, u32[]{:S(2)}, u32[]{:S(2)}) %collective-permute-start.15) | collective-permute-done | bytes 655392 | tf_op jit(solution)/shard_map/ppermute | solution.py:24
  171.0 11.4 %collective-permute-start.17 = (bf16[2,80,1024]{2,1,0:T(8,128)(2,1)S(1)}, bf16[2,80,1024]{2,1,0:T(8,128)(2,1)S(1)}, u32[]{:S(2)}, u32[]{:S(2)}) collective-permute-start(bf16[2,80,1024]{2,1,0:T(8,128)(2,1)S(1)} %fusion.24), channel_id=1, source_target_pairs={{0,1},{1,2},{2,3},{4,5},{5,6},{6,7},{8,9},{9,10},{10,11},{12,13},{... | collective-permute-start | bytes 983048 | tf_op jit(solution)/shard_map/ppermute | solution.py:24
  185.1 3.8 %collective-permute-done.17 = bf16[2,80,1024]{2,1,0:T(8,128)(2,1)S(1)} collective-permute-done((bf16[2,80,1024]{2,1,0:T(8,128)(2,1)S(1)}, bf16[2,80,1024]{2,1,0:T(8,128)(2,1)S(1)}, u32[]{:S(2)}, u32[]{:S(2)}) %collective-permute-start.17) | collective-permute-done | bytes 327712 | tf_op jit(solution)/shard_map/ppermute | solution.py:24
  189.6 6.3 %collective-permute-done.16 = bf16[2,80,1024]{2,1,0:T(8,128)(2,1)S(1)} collective-permute-done((bf16[2,80,1024]{2,1,0:T(8,128)(2,1)S(1)}, bf16[2,80,1024]{2,1,0:T(8,128)(2,1)S(1)}, u32[]{:S(2)}, u32[]{:S(2)}) %collective-permute-start.16) | collective-permute-done | bytes 327712 | tf_op jit(solution)/shard_map/ppermute | solution.py:24
  198.4 10.9 %collective-permute-done.45 = bf16[2,80,2048]{2,1,0:T(8,128)(2,1)S(1)} collective-permute-done((bf16[2,80,2048]{2,1,0:T(8,128)(2,1)S(1)}, bf16[2,80,2048]{2,1,0:T(8,128)(2,1)S(1)}, u32[]{:S(2)}, u32[]{:S(2)}) %collective-permute-start.45) | collective-permute-done | bytes 655392 | tf_op jit(solution)/shard_map/ppermute | solution.py:24
  211.6 2.9 fusion.8
  214.8 4.7 %collective-permute-start.47 = (bf16[80,1024]{1,0:T(8,128)(2,1)S(1)}, bf16[80,1024]{1,0:T(8,128)(2,1)S(1)}, u32[]{:S(2)}, u32[]{:S(2)}) collective-permute-start(bf16[80,1024]{1,0:T(8,128)(2,1)S(1)} %get-tuple-element.74), channel_id=1, source_target_pairs={{0,30},{1,31},{2,28},{3,29},{4,26},{5,27},{6,24},{7,25},{8,6},{9,7... | collective-permute-start | bytes 491528 | tf_op jit(solution)/shard_map/ppermute | solution.py:24
  219.5 2.6 collective-permute-start.48
  222.3 2.4 collective-permute-start.49
  224.7 2.1 collective-permute-start.50
  226.8 11.2 %collective-permute-start.51 = (bf16[80,1024]{1,0:T(8,128)(2,1)S(1)}, bf16[80,1024]{1,0:T(8,128)(2,1)S(1)}, u32[]{:S(2)}, u32[]{:S(2)}) collective-permute-start(bf16[80,1024]{1,0:T(8,128)(2,1)S(1)} %get-tuple-element.70), channel_id=1, source_target_pairs={{0,31},{1,28},{2,29},{3,30},{4,27},{5,24},{6,25},{7,26},{8,7},{9,4... | collective-permute-start | bytes 491528 | tf_op jit(solution)/shard_map/ppermute | solution.py:24
  246.2 2.5 collective-permute-done.53
  249.8 7.3 %collective-permute-done.21 = bf16[2,80,1024]{2,1,0:T(8,128)(2,1)S(1)} collective-permute-done((bf16[2,80,1024]{2,1,0:T(8,128)(2,1)S(1)}, bf16[2,80,1024]{2,1,0:T(8,128)(2,1)S(1)}, u32[]{:S(2)}, u32[]{:S(2)}) %collective-permute-start.21) | collective-permute-done | bytes 327712 | tf_op jit(solution)/shard_map/ppermute | solution.py:24
  259.1 3.4 %collective-permute-start.23 = (bf16[80,1024]{1,0:T(8,128)(2,1)S(1)}, bf16[80,1024]{1,0:T(8,128)(2,1)S(1)}, u32[]{:S(2)}, u32[]{:S(2)}) collective-permute-start(bf16[80,1024]{1,0:T(8,128)(2,1)S(1)} %get-tuple-element.82), channel_id=1, source_target_pairs={{0,14},{1,15},{2,12},{3,13},{4,10},{5,11},{6,8},{7,9},{8,22},{9,23... | collective-permute-start | bytes 491528 | tf_op jit(solution)/shard_map/ppermute | solution.py:24
  264.6 15.2 %collective-permute-done.22 = bf16[80,1024]{1,0:T(8,128)(2,1)S(1)} collective-permute-done((bf16[80,1024]{1,0:T(8,128)(2,1)S(1)}, bf16[80,1024]{1,0:T(8,128)(2,1)S(1)}, u32[]{:S(2)}, u32[]{:S(2)}) %collective-permute-start.22) | collective-permute-done | bytes 163872 | tf_op jit(solution)/shard_map/ppermute | solution.py:24
  279.8 3.6 %collective-permute-done.23 = bf16[80,1024]{1,0:T(8,128)(2,1)S(1)} collective-permute-done((bf16[80,1024]{1,0:T(8,128)(2,1)S(1)}, bf16[80,1024]{1,0:T(8,128)(2,1)S(1)}, u32[]{:S(2)}, u32[]{:S(2)}) %collective-permute-start.23) | collective-permute-done | bytes 163872 | tf_op jit(solution)/shard_map/ppermute | solution.py:24
  283.7 2.7 collective-permute-start.29
  287.5 3.5 %collective-permute-done.27 = bf16[80,1024]{1,0:T(8,128)(2,1)S(1)} collective-permute-done((bf16[80,1024]{1,0:T(8,128)(2,1)S(1)}, bf16[80,1024]{1,0:T(8,128)(2,1)S(1)}, u32[]{:S(2)}, u32[]{:S(2)}) %collective-permute-start.27) | collective-permute-done | bytes 163872 | tf_op jit(solution)/shard_map/ppermute | solution.py:24
  291.0 3.3 %collective-permute-done.29 = bf16[80,1024]{1,0:T(8,128)(2,1)S(1)} collective-permute-done((bf16[80,1024]{1,0:T(8,128)(2,1)S(1)}, bf16[80,1024]{1,0:T(8,128)(2,1)S(1)}, u32[]{:S(2)}, u32[]{:S(2)}) %collective-permute-start.29) | collective-permute-done | bytes 163872 | tf_op jit(solution)/shard_map/ppermute | solution.py:24
  (176 shorter events, 85.6 us)
Async XLA Ops:
  12.0 21.7 %collective-permute-start.4 = (bf16[128,1024]{1,0:T(8,128)(2,1)}, bf16[128,1024]{1,0:T(8,128)(2,1)}, u32[]{:S(2)}, u32[]{:S(2)}) collective-permute-start(bf16[128,1024]{1,0:T(8,128)(2,1)} %convolution_convert_fusion.2), channel_id=1, source_target_pairs={{0,2},{1,3},{2,0},{3,1},{4,6},{5,7},{6,4},{7,5},{8,10},{9,11},{10,... | collective-permute-start | bytes 786440 | tf_op jit(solution)/shard_map/ppermute | solution.py:24
  13.0 20.8 %collective-permute-start.5 = (bf16[128,1024]{1,0:T(8,128)(2,1)}, bf16[128,1024]{1,0:T(8,128)(2,1)}, u32[]{:S(2)}, u32[]{:S(2)}) collective-permute-start(bf16[128,1024]{1,0:T(8,128)(2,1)} %convolution_convert_fusion.1), channel_id=1, source_target_pairs={{0,1},{1,2},{2,3},{3,0},{4,5},{5,6},{6,7},{7,4},{8,9},{9,10},{10,1... | collective-permute-start | bytes 786440 | tf_op jit(solution)/shard_map/ppermute | solution.py:24
  33.8 32.7 %collective-permute-start.7 = (bf16[128,1024]{1,0:T(8,128)(2,1)}, bf16[128,1024]{1,0:T(8,128)(2,1)S(1)}, u32[]{:S(2)}, u32[]{:S(2)}) collective-permute-start(bf16[128,1024]{1,0:T(8,128)(2,1)} %convolution_convert_fusion.6), channel_id=1, source_target_pairs={{0,2},{1,3},{2,0},{3,1},{4,6},{5,7},{6,4},{7,5},{8,10},{9,11},{10,... | collective-permute-start | bytes 786440 | tf_op jit(solution)/shard_map/ppermute | solution.py:24
  42.9 23.5 %collective-permute-start.8 = (bf16[128,1024]{1,0:T(8,128)(2,1)}, bf16[128,1024]{1,0:T(8,128)(2,1)S(1)}, u32[]{:S(2)}, u32[]{:S(2)}) collective-permute-start(bf16[128,1024]{1,0:T(8,128)(2,1)} %convolution_convert_fusion.5), channel_id=1, source_target_pairs={{0,1},{1,2},{2,3},{3,0},{4,5},{5,6},{6,7},{7,4},{8,9},{9,10},{10,1... | collective-permute-start | bytes 786440 | tf_op jit(solution)/shard_map/ppermute | solution.py:24
  46.3 21.9 %collective-permute-start.32 = (bf16[4,80,1024]{2,1,0:T(8,128)(2,1)S(1)}, bf16[4,80,1024]{2,1,0:T(8,128)(2,1)S(1)}, u32[]{:S(2)}, u32[]{:S(2)}) collective-permute-start(bf16[4,80,1024]{2,1,0:T(8,128)(2,1)S(1)} %get-tuple-element.87), channel_id=1, source_target_pairs={{0,4},{1,5},{2,6},{3,7},{4,0},{5,1},{6,2},{7,3},{8,12},{9,13},{10,... | collective-permute-start | bytes 1966088 | tf_op jit(solution)/shard_map/ppermute | solution.py:24
  71.2 20.6 %collective-permute-start.33 = (bf16[2,80,1024]{2,1,0:T(8,128)(2,1)S(1)}, bf16[2,80,1024]{2,1,0:T(8,128)(2,1)S(1)}, u32[]{:S(2)}, u32[]{:S(2)}) collective-permute-start(bf16[2,80,1024]{2,1,0:T(8,128)(2,1)S(1)} %convert_element_type.209), channel_id=1, source_target_pairs={{0,1},{4,5},{8,9},{12,13},{16,17},{20,21},{24,25},{28,29}} | collective-permute-start | bytes 983048 | tf_op jit(solution)/shard_map/ppermute | solution.py:24
  72.6 19.3 %collective-permute-start.36 = (bf16[2,80,1024]{2,1,0:T(8,128)(2,1)S(1)}, bf16[2,80,1024]{2,1,0:T(8,128)(2,1)S(1)}, u32[]{:S(2)}, u32[]{:S(2)}) collective-permute-start(bf16[2,80,1024]{2,1,0:T(8,128)(2,1)S(1)} %convert_element_type.215), channel_id=1, source_target_pairs={{3,2},{7,6},{11,10},{15,14},{19,18},{23,22},{27,26},{31,30}} | collective-permute-start | bytes 983048 | tf_op jit(solution)/shard_map/ppermute | solution.py:24
  89.7 29.5 %collective-permute-start.10 = (bf16[2,80,2048]{2,1,0:T(8,128)(2,1)S(1)}, bf16[2,80,2048]{2,1,0:T(8,128)(2,1)S(1)}, u32[]{:S(2)}, u32[]{:S(2)}) collective-permute-start(bf16[2,80,2048]{2,1,0:T(8,128)(2,1)S(1)} %convert_element_type.191), channel_id=1, source_target_pairs={{0,1},{4,5},{8,9},{12,13},{16,17},{20,21},{24,25},{28,29}} | collective-permute-start | bytes 1966088 | tf_op jit(solution)/shard_map/ppermute | solution.py:24
  91.1 28.1 %collective-permute-start.13 = (bf16[2,80,2048]{2,1,0:T(8,128)(2,1)S(1)}, bf16[2,80,2048]{2,1,0:T(8,128)(2,1)S(1)}, u32[]{:S(2)}, u32[]{:S(2)}) collective-permute-start(bf16[2,80,2048]{2,1,0:T(8,128)(2,1)S(1)} %convert_element_type.197), channel_id=1, source_target_pairs={{3,2},{7,6},{11,10},{15,14},{19,18},{23,22},{27,26},{31,30}} | collective-permute-start | bytes 1966088 | tf_op jit(solution)/shard_map/ppermute | solution.py:24
  92.1 19.0 %collective-permute-start.34 = (bf16[2,80,1024]{2,1,0:T(8,128)(2,1)S(1)}, bf16[2,80,1024]{2,1,0:T(8,128)(2,1)S(1)}, u32[]{:S(2)}, u32[]{:S(2)}) collective-permute-start(bf16[2,80,1024]{2,1,0:T(8,128)(2,1)S(1)} %get-tuple-element.90), channel_id=1, source_target_pairs={{0,1},{1,2},{4,5},{5,6},{8,9},{9,10},{12,13},{13,14},{16,17},{17,1... | collective-permute-start | bytes 983048 | tf_op jit(solution)/shard_map/ppermute | solution.py:24
  93.4 23.6 %collective-permute-start.37 = (bf16[2,80,1024]{2,1,0:T(8,128)(2,1)S(1)}, bf16[2,80,1024]{2,1,0:T(8,128)(2,1)S(1)}, u32[]{:S(2)}, u32[]{:S(2)}) collective-permute-start(bf16[2,80,1024]{2,1,0:T(8,128)(2,1)S(1)} %get-tuple-element.91), channel_id=1, source_target_pairs={{2,1},{3,2},{6,5},{7,6},{10,9},{11,10},{14,13},{15,14},{18,17},{19... | collective-permute-start | bytes 983048 | tf_op jit(solution)/shard_map/ppermute | solution.py:24
  95.0 31.0 %collective-permute-start.39 = (bf16[80,2048]{1,0:T(8,128)(2,1)}, bf16[80,2048]{1,0:T(8,128)(2,1)}, u32[]{:S(2)}, u32[]{:S(2)}) collective-permute-start(bf16[80,2048]{1,0:T(8,128)(2,1)} %get-tuple-element.93), channel_id=1, source_target_pairs={{0,4},{1,5},{2,6},{3,7},{4,0},{5,1},{6,2},{7,3},{8,12},{9,13},{10,... | collective-permute-start | bytes 983048 | tf_op jit(solution)/shard_map/ppermute | solution.py:24
  120.6 19.1 %collective-permute-start.11 = (bf16[2,80,2048]{2,1,0:T(8,128)(2,1)}, bf16[2,80,2048]{2,1,0:T(8,128)(2,1)}, u32[]{:S(2)}, u32[]{:S(2)}) collective-permute-start(bf16[2,80,2048]{2,1,0:T(8,128)(2,1)} %get-tuple-element.84), channel_id=1, source_target_pairs={{0,1},{1,2},{4,5},{5,6},{8,9},{9,10},{12,13},{13,14},{16,17},{17,1... | collective-permute-start | bytes 1966088 | tf_op jit(solution)/shard_map/ppermute | solution.py:24
  126.0 22.3 %collective-permute-start.31 = (s32[128]{0:T(128)S(1)}, s32[128]{0:T(128)S(1)}, u32[]{:S(2)}, u32[]{:S(2)}) collective-permute-start(s32[128]{0:T(128)S(1)} %bitcast.195), channel_id=1, source_target_pairs={{0,24},{1,25},{2,26},{3,27},{4,28},{5,29},{6,30},{7,31},{8,0},{9,1... | collective-permute-start | bytes 1544 | tf_op jit(solution)/shard_map/ppermute | solution.py:24
  126.0 24.9 %collective-permute-start.2 = (s32[128]{0:T(128)S(1)}, s32[128]{0:T(128)S(1)}, u32[]{:S(2)}, u32[]{:S(2)}) collective-permute-start(s32[128]{0:T(128)S(1)} %bitcast.196), channel_id=1, source_target_pairs={{0,8},{1,9},{2,10},{3,11},{4,12},{5,13},{6,14},{7,15},{8,16},{9,17... | collective-permute-start | bytes 1544 | tf_op jit(solution)/shard_map/ppermute | solution.py:24
  130.9 22.9 %collective-permute-start.41 = (bf16[2,80,2048]{2,1,0:T(8,128)(2,1)}, bf16[2,80,2048]{2,1,0:T(8,128)(2,1)}, u32[]{:S(2)}, u32[]{:S(2)}) collective-permute-start(bf16[2,80,2048]{2,1,0:T(8,128)(2,1)} %pad_maximum_fusion.6), channel_id=1, source_target_pairs={{0,1},{1,2},{2,3},{4,5},{5,6},{6,7},{8,9},{9,10},{10,11},{12,13},{... | collective-permute-start | bytes 1966088 | tf_op jit(solution)/shard_map/ppermute | solution.py:24
  143.1 22.0 %collective-permute-start.12 = (bf16[2,80,2048]{2,1,0:T(8,128)(2,1)}, bf16[2,80,2048]{2,1,0:T(8,128)(2,1)S(1)}, u32[]{:S(2)}, u32[]{:S(2)}) collective-permute-start(bf16[2,80,2048]{2,1,0:T(8,128)(2,1)} %add_convert_fusion.4), channel_id=1, source_target_pairs={{0,1},{1,2},{2,3},{4,5},{5,6},{6,7},{8,9},{9,10},{10,11},{12,13},{... | collective-permute-start | bytes 1966088 | tf_op jit(solution)/shard_map/ppermute | solution.py:24
  148.3 19.8 %collective-permute-start.15 = (bf16[2,80,2048]{2,1,0:T(8,128)(2,1)S(1)}, bf16[2,80,2048]{2,1,0:T(8,128)(2,1)}, u32[]{:S(2)}, u32[]{:S(2)}) collective-permute-start(bf16[2,80,2048]{2,1,0:T(8,128)(2,1)S(1)} %add_convert_fusion.2), channel_id=1, source_target_pairs={{1,0},{2,1},{3,2},{5,4},{6,5},{7,6},{9,8},{10,9},{11,10},{13,12},{... | collective-permute-start | bytes 1966088 | tf_op jit(solution)/shard_map/ppermute | solution.py:24
  154.6 29.1 %collective-permute-start.44 = (bf16[2,80,2048]{2,1,0:T(8,128)(2,1)}, bf16[2,80,2048]{2,1,0:T(8,128)(2,1)S(1)}, u32[]{:S(2)}, u32[]{:S(2)}) collective-permute-start(bf16[2,80,2048]{2,1,0:T(8,128)(2,1)} %collective-permute-done.40), channel_id=1, source_target_pairs={{1,0},{2,1},{5,4},{6,5},{9,8},{10,9},{13,12},{14,13},{17,16},{18,1... | collective-permute-start | bytes 1966088 | tf_op jit(solution)/shard_map/ppermute | solution.py:24
  169.9 27.3 %collective-permute-start.43 = (bf16[2,80,2048]{2,1,0:T(8,128)(2,1)S(1)}, bf16[2,80,2048]{2,1,0:T(8,128)(2,1)S(1)}, u32[]{:S(2)}, u32[]{:S(2)}) collective-permute-start(bf16[2,80,2048]{2,1,0:T(8,128)(2,1)S(1)} %collective-permute-done.42), channel_id=1, source_target_pairs={{2,3},{6,7},{10,11},{14,15},{18,19},{22,23},{26,27},{30,31}} | collective-permute-start | bytes 1966088 | tf_op jit(solution)/shard_map/ppermute | solution.py:24
  183.7 25.6 %collective-permute-start.45 = (bf16[2,80,2048]{2,1,0:T(8,128)(2,1)S(1)}, bf16[2,80,2048]{2,1,0:T(8,128)(2,1)S(1)}, u32[]{:S(2)}, u32[]{:S(2)}) collective-permute-start(bf16[2,80,2048]{2,1,0:T(8,128)(2,1)S(1)} %collective-permute-done.44), channel_id=1, source_target_pairs={{1,0},{5,4},{9,8},{13,12},{17,16},{21,20},{25,24},{29,28}} | collective-permute-start | bytes 1966088 | tf_op jit(solution)/shard_map/ppermute | solution.py:24
  188.9 33.3 %collective-permute-start.18 = (bf16[2,80,1024]{2,1,0:T(8,128)(2,1)S(1)}, bf16[2,80,1024]{2,1,0:T(8,128)(2,1)S(1)}, u32[]{:S(2)}, u32[]{:S(2)}) collective-permute-start(bf16[2,80,1024]{2,1,0:T(8,128)(2,1)S(1)} %collective-permute-done.17), channel_id=1, source_target_pairs={{1,2},{2,3},{5,6},{6,7},{9,10},{10,11},{13,14},{14,15},{17,18},{18... | collective-permute-start | bytes 983048 | tf_op jit(solution)/shard_map/ppermute | solution.py:24
  195.9 28.8 %collective-permute-start.20 = (bf16[2,80,1024]{2,1,0:T(8,128)(2,1)S(1)}, bf16[2,80,1024]{2,1,0:T(8,128)(2,1)S(1)}, u32[]{:S(2)}, u32[]{:S(2)}) collective-permute-start(bf16[2,80,1024]{2,1,0:T(8,128)(2,1)S(1)} %collective-permute-done.16), channel_id=1, source_target_pairs={{1,0},{2,1},{5,4},{6,5},{9,8},{10,9},{13,12},{14,13},{17,16},{18,1... | collective-permute-start | bytes 983048 | tf_op jit(solution)/shard_map/ppermute | solution.py:24
  214.8 24.2 %collective-permute-start.47 = (bf16[80,1024]{1,0:T(8,128)(2,1)S(1)}, bf16[80,1024]{1,0:T(8,128)(2,1)S(1)}, u32[]{:S(2)}, u32[]{:S(2)}) collective-permute-start(bf16[80,1024]{1,0:T(8,128)(2,1)S(1)} %get-tuple-element.74), channel_id=1, source_target_pairs={{0,30},{1,31},{2,28},{3,29},{4,26},{5,27},{6,24},{7,25},{8,6},{9,7... | collective-permute-start | bytes 491528 | tf_op jit(solution)/shard_map/ppermute | solution.py:24
  219.5 20.4 %collective-permute-start.48 = (bf16[80,1024]{1,0:T(8,128)(2,1)S(1)}, bf16[80,1024]{1,0:T(8,128)(2,1)S(1)}, u32[]{:S(2)}, u32[]{:S(2)}) collective-permute-start(bf16[80,1024]{1,0:T(8,128)(2,1)S(1)} %get-tuple-element.73), channel_id=1, source_target_pairs={{0,25},{1,26},{2,27},{3,24},{4,29},{5,30},{6,31},{7,28},{8,1},{9,2... | collective-permute-start | bytes 491528 | tf_op jit(solution)/shard_map/ppermute | solution.py:24
  222.3 19.2 %collective-permute-start.49 = (bf16[80,1024]{1,0:T(8,128)(2,1)S(1)}, bf16[80,1024]{1,0:T(8,128)(2,1)S(1)}, u32[]{:S(2)}, u32[]{:S(2)}) collective-permute-start(bf16[80,1024]{1,0:T(8,128)(2,1)S(1)} %get-tuple-element.72), channel_id=1, source_target_pairs={{0,29},{1,30},{2,31},{3,28},{4,25},{5,26},{6,27},{7,24},{8,5},{9,6... | collective-permute-start | bytes 491528 | tf_op jit(solution)/shard_map/ppermute | solution.py:24
  241.5 21.7 %collective-permute-start.30 = (bf16[128,4096]{1,0:T(8,128)(2,1)S(1)}, bf16[128,4096]{1,0:T(8,128)(2,1)S(1)}, u32[]{:S(2)}, u32[]{:S(2)}) collective-permute-start(bf16[128,4096]{1,0:T(8,128)(2,1)S(1)} %bitcast.185), channel_id=1, source_target_pairs={{0,24},{1,25},{2,26},{3,27},{4,28},{5,29},{6,30},{7,31},{8,0},{9,1... | collective-permute-start | bytes 3145736 | tf_op jit(solution)/shard_map/ppermute | solution.py:24
  259.0 20.8 %collective-permute-start.22 = (bf16[80,1024]{1,0:T(8,128)(2,1)S(1)}, bf16[80,1024]{1,0:T(8,128)(2,1)S(1)}, u32[]{:S(2)}, u32[]{:S(2)}) collective-permute-start(bf16[80,1024]{1,0:T(8,128)(2,1)S(1)} %get-tuple-element.83), channel_id=1, source_target_pairs={{0,10},{1,11},{2,8},{3,9},{4,14},{5,15},{6,12},{7,13},{8,18},{9,19... | collective-permute-start | bytes 491528 | tf_op jit(solution)/shard_map/ppermute | solution.py:24
  259.1 24.3 %collective-permute-start.23 = (bf16[80,1024]{1,0:T(8,128)(2,1)S(1)}, bf16[80,1024]{1,0:T(8,128)(2,1)S(1)}, u32[]{:S(2)}, u32[]{:S(2)}) collective-permute-start(bf16[80,1024]{1,0:T(8,128)(2,1)S(1)} %get-tuple-element.82), channel_id=1, source_target_pairs={{0,14},{1,15},{2,12},{3,13},{4,10},{5,11},{6,8},{7,9},{8,22},{9,23... | collective-permute-start | bytes 491528 | tf_op jit(solution)/shard_map/ppermute | solution.py:24
  262.5 20.9 %collective-permute-start.24 = (bf16[80,1024]{1,0:T(8,128)(2,1)S(1)}, bf16[80,1024]{1,0:T(8,128)(2,1)S(1)}, u32[]{:S(2)}, u32[]{:S(2)}) collective-permute-start(bf16[80,1024]{1,0:T(8,128)(2,1)S(1)} %get-tuple-element.81), channel_id=1, source_target_pairs={{0,9},{1,10},{2,11},{3,8},{4,13},{5,14},{6,15},{7,12},{8,17},{9,18... | collective-permute-start | bytes 491528 | tf_op jit(solution)/shard_map/ppermute | solution.py:24
  262.5 21.2 %collective-permute-start.25 = (bf16[80,1024]{1,0:T(8,128)(2,1)S(1)}, bf16[80,1024]{1,0:T(8,128)(2,1)S(1)}, u32[]{:S(2)}, u32[]{:S(2)}) collective-permute-start(bf16[80,1024]{1,0:T(8,128)(2,1)S(1)} %get-tuple-element.80), channel_id=1, source_target_pairs={{0,13},{1,14},{2,15},{3,12},{4,9},{5,10},{6,11},{7,8},{8,21},{9,22... | collective-permute-start | bytes 491528 | tf_op jit(solution)/shard_map/ppermute | solution.py:24
  263.2 32.4 %collective-permute-start = (bf16[128,4096]{1,0:T(8,128)(2,1)S(1)}, bf16[128,4096]{1,0:T(8,128)(2,1)S(1)}, u32[]{:S(2)}, u32[]{:S(2)}) collective-permute-start(bf16[128,4096]{1,0:T(8,128)(2,1)S(1)} %bitcast.186), channel_id=1, source_target_pairs={{0,8},{1,9},{2,10},{3,11},{4,12},{5,13},{6,14},{7,15},{8,16},{9,17... | collective-permute-start | bytes 3145736 | tf_op jit(solution)/shard_map/ppermute | solution.py:24
  (37 other events, 479.6 us)
where the time goes:
time: 298 us; the launch traced here: 297 us
  waiting for transfers between devices  133 us (45%)
  starting transfers between devices  106 us (36%)
  other arithmetic  22.5 us (8%)
  matrix products  22.5 us (8%)
  local copies, waits for them, and re-layouts  8.18 us (3%)
  between operations  4.1 us (1%)
    ppermute x54, waiting for transfers between devices, move(): return lax.ppermute(value, AXES, pairs)  133 us
    ppermute x54, starting transfers between devices, move(): return lax.ppermute(value, AXES, pairs)  106 us
    dot_general x8, matrix products, to_owners(): jnp.dot(placer, block, preferred_element_type=F32).astype(BF16)  9.84 us
  transfers between devices with their start and end apart: 54, of which 20 were waited for; matrix products, arithmetic and copies ran while one was open for 14% of the time, Pallas kernels for 0%

commit v1 on v0

--- a/solution.py
+++ b/solution.py
@@ -68,55 +68,75 @@
     return lax.optimization_barrier(values)
 
 
-def to_owners(tokens, placer, local, after=()):
+def after(values, *others):
+    return list(join(*values, *others)[: len(values)])
+
+
+def cut(tokens, placer, local):
     column = tokens.shape[1] // 4
     blocks = []
     for m in range(4):
         block = lax.dynamic_slice_in_dim(tokens, ((local - m) % 4) * column, column, axis=1)
         blocks.append(jnp.dot(placer, block, preferred_element_type=F32).astype(BF16))
-    if after:
-        blocks = join(*blocks, *after)[:4]
-    return join(blocks[0], *(move(blocks[m], by_local=-m) for m in (1, 2, 3)))
-
-
-def to_expert(blocks, node, capacity):
-    own, other = windows(jnp.stack(blocks), node, capacity)
-    got = move(other, by_node=1)
-    return jnp.stack([own, got], axis=1)
-
-
-def reduce_scatter(partial):
+    return blocks
+
+
+def sums(partial):
     right, left = partial[3], partial[1]
     for step in (1, 2, 3):
-        got_r = move(right.astype(BF16), by_local=1, wrap=False, last=step - 1)
-        got_l = move(left.astype(BF16), by_local=-1, wrap=False, first=4 - step)
+        right, left = right.astype(BF16), left.astype(BF16)
+        got_r, got_l = yield (
+            (right, dict(by_local=1, wrap=False, last=step - 1)),
+            (left, dict(by_local=-1, wrap=False, first=4 - step)),
+        )
         right = partial[3 - step] + got_r.astype(F32)
         if step < 3:
             left = partial[step + 1] + got_l.astype(F32)
-    return right + got_l.astype(F32)
-
-
-def all_gather(rows, local):
+    yield right + got_l.astype(F32)
+
+
+def gathers(rows, local):
     from_left, from_right = [rows], [rows]
     for step in (1, 2, 3):
-        from_left.append(move(from_left[-1], by_local=1, wrap=False, first=step - 1))
-        from_right.append(move(from_right[-1], by_local=-1, wrap=False, last=4 - step))
+        got_r, got_l = yield (
+            (from_left[-1], dict(by_local=1, wrap=False, first=step - 1)),
+            (from_right[-1], dict(by_local=-1, wrap=False, last=4 - step)),
+        )
+        from_left.append(got_r)
+        from_right.append(got_l)
     slots = [rows]
     for m in (1, 2, 3):
         slots.append(jnp.where(local + m < 4, from_right[m], from_left[4 - m]))
-    return jnp.stack(slots)
-
-
-def give_back(done, by_pp):
-    got = []
+    yield jnp.stack(slots)
+
+
+def send(pieces):
+    return [move(value, **how) for value, how in pieces]
+
+
+def operands(pieces):
+    return [value for value, _ in pieces]
+
+
+def returns(done, by_pp):
+    pieces = []
     for m in (2, 1, 3, 0):
-        got.append(move(done[m, 0], by_pp=by_pp, by_local=m))
-        got.append(move(done[m, 1], by_pp=by_pp, by_node=1, by_local=m))
+        pieces.append((done[m, 0], dict(by_pp=by_pp, by_local=m)))
+        pieces.append((done[m, 1], dict(by_pp=by_pp, by_node=1, by_local=m)))
+    return pieces
+
+
+def at_home(got):
     got = join(*got)
     rows = [None] * 4
     for i, m in enumerate((2, 1, 3, 0)):
         rows[m] = jnp.concatenate([got[2 * i], got[2 * i + 1]], axis=0)
     return rows
+
+
+def later(pieces, *others):
+    values = after(operands(pieces), *others)
+    return [(value, how) for value, (_, how) in zip(values, pieces)]
 
 
 def unsort(blocks, placer, local):
@@ -140,55 +160,105 @@
     w_gu = w_gate_up[0, 0]
     w_dn = w_down[0, 0]
     hidden_units = w_dn.shape[0]
-
-    act = act_fwd[0]
-    grad = grad_bwd[0]
-    sort_a = sorter(routes_fwd[0, :, 0])
-    sort_b = sorter(routes_bwd[0, :, 0])
+    shape = (4, 2, capacity)
+
+    act, grad = act_fwd[0], grad_bwd[0]
+    route_a, route_b = routes_fwd[0, :, 0], routes_bwd[0, :, 0]
+    sort_b, sort_a = sorter(route_b), sorter(route_a)
+
     dy = (weight_bwd[0][:, None] * grad.astype(F32)).astype(BF16)
-    blocks_b = to_owners(dy, sort_b, local)
-    blocks_a = to_owners(act, sort_a, local, after=blocks_b[1:])
-    rows_b = to_expert(blocks_b, node, capacity)
-    rows_a = to_expert(blocks_a, node, capacity)
+    cut_b = cut(dy, sort_b, local)
+    cut_a = cut(act, sort_a, local)
+    got_b = [move(cut_b[m], by_local=-m) for m in (2, 1, 3)]
+    grad_next = move(grad, by_pp=-1)
+    route_b_next = move(route_b, by_pp=-1)
     saved = jnp.dot(sort_b, saved_bwd[0], preferred_element_type=F32).astype(BF16)
     saved_own, saved_other = windows(saved, node, capacity)
-    saved_rows = jnp.stack([saved_own, move(saved_other, by_node=1)])
-
+    saved_got = move(saved_other, by_node=1)
+    got_a2 = move(cut_a[2], by_local=-2)
+    *got_b, grad_next, route_b_next, saved_got = join(*got_b, grad_next, route_b_next, saved_got)
+    cut_a1, cut_a3 = after([cut_a[1], cut_a[3]], *got_b)
+    got_a = [got_a2, move(cut_a1, by_local=-1), move(cut_a3, by_local=-3)]
     act_next = move(act, by_pp=1)
-    grad_next = move(grad, by_pp=-1)
-    route_a_next = move(routes_fwd[0, :, 0], by_pp=1)
-    route_b_next = move(routes_bwd[0, :, 0], by_pp=-1)
-    weight_next = move(weight_fwd[0], by_pp=1)
-
-    shape = (4, 2, capacity)
-    column = rows_a.shape[-1]
-    part_a = jnp.dot(rows_a.reshape(-1, column), w_gu, preferred_element_type=F32)
-    preact = reduce_scatter(part_a.reshape(shape + (2 * hidden_units,)))
-    part_b = dot_t(rows_b.reshape(-1, column), w_dn)
-    dh = reduce_scatter(part_b.reshape(shape + (hidden_units,)))
-
-    hidden = (jax.nn.silu(preact[..., :hidden_units]) * preact[..., hidden_units:]).astype(BF16)
-    all_hidden = all_gather(hidden, local)
-    done_a = jnp.dot(
-        all_hidden.reshape(-1, hidden_units), w_dn, preferred_element_type=F32
-    ).astype(BF16)
-
+    small_next = move(jnp.stack([route_a.astype(F32), weight_fwd[0]]), by_pp=1)
+
+    def to_expert(blocks):
+        own, other = windows(jnp.stack(blocks), node, capacity)
+        return own, other
+
+    def expert_rows(own, got):
+        rows = jnp.stack([own, got], axis=1)
+        return rows.reshape(-1, rows.shape[-1])
+
+    own_b, other_b = to_expert([cut_b[0], got_b[1], got_b[0], got_b[2]])
+    got_bx = move(other_b, by_node=1)
+    part_b = dot_t(expert_rows(own_b, got_bx), w_dn).reshape(shape + (hidden_units,))
+    chain_b = sums(part_b)
+    pieces_b = next(chain_b)
+    back_b = send(pieces_b)
+
+    *got_a, act_next, small_next = join(*got_a, act_next, small_next)
+    own_a, other_a = to_expert([cut_a[0], got_a[1], got_a[0], got_a[2]])
+    (got_ax,) = after([move(other_a, by_node=1)], *operands(pieces_b))
+    back_b = after(back_b, other_a)
+    pieces_b = chain_b.send(back_b)
+    back_b = send(pieces_b)
+    (got_ax,) = after([got_ax], *operands(pieces_b))
+    part_a = jnp.dot(expert_rows(own_a, got_ax), w_gu, preferred_element_type=F32)
+    chain_a = sums(part_a.reshape(shape + (2 * hidden_units,)))
+    pieces_a = next(chain_a)
+    back_a = send(pieces_a)
+    back_b = after(back_b, *operands(pieces_a))
+    pieces_b = chain_b.send(back_b)
+    back_b = send(pieces_b)
+    dh = chain_b.send(back_b)
+
+    saved_rows = jnp.stack([saved_own, saved_got])
     g = saved_rows[..., :hidden_units].astype(F32)
     u = saved_rows[..., hidden_units:].astype(F32)
     q = 1.0 / (1.0 + jnp.exp(-g))
     grad_gu = jnp.concatenate([dh * u * q * (1.0 + g * (1.0 - q)), dh * g * q], axis=-1).astype(
         BF16
     )
-    all_gu = all_gather(grad_gu, local)
+    chain_b = gathers(grad_gu, local)
+    pieces_b = next(chain_b)
+    back_b = send(pieces_b)
+    for _ in (2, 3):
+        back_a = after(back_a, *operands(pieces_b))
+        pieces_a = chain_a.send(back_a)
+        back_a = send(pieces_a)
+        back_b = after(back_b, *operands(pieces_a))
+        pieces_b = chain_b.send(back_b)
+        back_b = send(pieces_b)
+    back_a = after(back_a, *operands(pieces_b))
+    preact = chain_a.send(back_a)
+    hidden = (jax.nn.silu(preact[..., :hidden_units]) * preact[..., hidden_units:]).astype(BF16)
+    chain_a = gathers(hidden, local)
+    pieces_a = next(chain_a)
+    back_a = send(pieces_a)
+    back_b = after(back_b, *operands(pieces_a))
+    all_gu = chain_b.send(back_b)
     done_b = dot_t(all_gu.reshape(-1, 2 * hidden_units), w_gu).astype(BF16)
-
-    back_a = give_back(done_a.reshape(shape + (column,)), 1)
-    back_b = give_back(done_b.reshape(shape + (column,)), -1)
-
-    moe_a = unsort(back_a, window_placer(route_a_next, node, capacity), local)
-    next_input = (act_next.astype(F32) + weight_next[:, None] * moe_a).astype(BF16)
-    moe_b = unsort(back_b, window_placer(route_b_next, node, capacity), local)
+    done_b = done_b.reshape(shape + (done_b.shape[-1],))
+    out_b = returns(done_b, -1)
+    home_b = send(out_b[:3])
+    for group in (out_b[3:6], out_b[6:]):
+        pieces_a = chain_a.send(after(back_a, done_b))
+        back_a = send(pieces_a)
+        home_b += send(later(group, *operands(pieces_a)))
+    all_hidden = chain_a.send(back_a)
+    done_a = jnp.dot(
+        all_hidden.reshape(-1, hidden_units), w_dn, preferred_element_type=F32
+    ).astype(BF16)
+    done_a = done_a.reshape(shape + (done_a.shape[-1],))
+
+    home_a = send(returns(done_a, 1))
+
+    moe_b = unsort(at_home(home_b), window_placer(route_b_next, node, capacity), local)
     prev_grad = (grad_next.astype(F32) + moe_b).astype(BF16)
+    route_a_next = small_next[0].astype(jnp.int32)
+    moe_a = unsort(at_home(home_a), window_placer(route_a_next, node, capacity), local)
+    next_input = (act_next.astype(F32) + small_next[1][:, None] * moe_a).astype(BF16)
     return next_input[None], prev_grad[None]
 
 

time: 298 us -> 285 us (0.956)
  waiting for transfers between devices: 133 us -> 110 us
  starting transfers between devices: 106 us -> 114 us
  other arithmetic: 22.5 us -> 25.7 us
    ppermute x54 -> x53, waiting for transfers between devices: 133 us -> 110 us  [move(): return lax.ppermute(value, AXES, pairs)]
    ppermute x54 -> x53, starting transfers between devices: 106 us -> 114 us  [move(): return lax.ppermute(value, AXES, pairs)]
    convert_element_type x10 -> x11, other arithmetic: 5.66 us -> 6.52 us  [the longest x10 6.51 us: sums(): right, left = (right.astype(BF16), left.astype(BF16))]
  transfers between devices with their start and end apart: 54 -> 53, of which waited for: 20 -> 21; matrix products, arithmetic and copies ran while one was open for 14% -> 15% of each run, Pallas kernels for 0% -> 0%
where the time goes in v1:
time: 285 us; the launch traced here: 284 us
  starting transfers between devices  114 us (40%)
  waiting for transfers between devices  110 us (39%)
  other arithmetic  25.7 us (9%)
  matrix products  22.9 us (8%)
  local copies, waits for them, and re-layouts  7.46 us (3%)
  between operations  4.02 us (1%)
    ppermute x53, starting transfers between devices, move(): return lax.ppermute(value, AXES, pairs)  114 us
    ppermute x53, waiting for transfers between devices, move(): return lax.ppermute(value, AXES, pairs)  110 us
    dot_general x8, matrix products, cut(): jnp.dot(placer, block, preferred_element_type=F32).astype(BF16)  8.43 us
    convert_element_type x10, other arithmetic, sums(): right, left = (right.astype(BF16), left.astype(BF16))  6.51 us
  transfers between devices with their start and end apart: 53, of which 21 were waited for; matrix products, arithmetic and copies ran while one was open for 15% of the time, Pallas kernels for 0%

profile of v1, /device:TPU:0, one launch (start us, length us, event | category | flops | bytes accessed | tf_op | source)
XLA Modules:
  0.0 283.7 jit_solution(9664954127533935083)
XLA Ops:
  5.4 4.1 %collective-permute-start.1 = (bf16[128,1024]{1,0:T(8,128)(2,1)S(1)}, bf16[128,1024]{1,0:T(8,128)(2,1)}, u32[]{:S(2)}, u32[]{:S(2)}) collective-permute-start(bf16[128,1024]{1,0:T(8,128)(2,1)S(1)} %convolution_convert_fusion.5), channel_id=1, source_target_pairs={{0,2},{1,3},{2,0},{3,1},{4,6},{5,7},{6,4},{7,5},{8,10},{9,11},{10,... | collective-permute-start | bytes 786440 | tf_op jit(solution)/shard_map/ppermute | solution.py:24
  23.0 11.8 %collective-permute-done.5 = s32[128]{0:T(128)S(1)} collective-permute-done((s32[128]{0:T(128)S(1)}, s32[128]{0:T(128)S(1)}, u32[]{:S(2)}, u32[]{:S(2)}) %collective-permute-start.5) | collective-permute-done | bytes 544 | tf_op jit(solution)/shard_map/ppermute | solution.py:24
  39.3 6.5 %collective-permute-done.3 = bf16[128,1024]{1,0:T(8,128)(2,1)S(1)} collective-permute-done((bf16[128,1024]{1,0:T(8,128)(2,1)}, bf16[128,1024]{1,0:T(8,128)(2,1)S(1)}, u32[]{:S(2)}, u32[]{:S(2)}) %collective-permute-start.3) | collective-permute-done | bytes 262176 | tf_op jit(solution)/shard_map/ppermute | solution.py:24
  46.2 3.0 %collective-permute-start.7 = (bf16[128,1024]{1,0:T(8,128)(2,1)S(1)}, bf16[128,1024]{1,0:T(8,128)(2,1)S(1)}, u32[]{:S(2)}, u32[]{:S(2)}) collective-permute-start(bf16[128,1024]{1,0:T(8,128)(2,1)S(1)} %copy-done.7), channel_id=1, source_target_pairs={{0,3},{1,0},{2,1},{3,2},{4,7},{5,4},{6,5},{7,6},{8,11},{9,8},{10,9... | collective-permute-start | bytes 786440 | tf_op jit(solution)/shard_map/ppermute | solution.py:24
  53.2 4.1 %collective-permute-done = bf16[128,1024]{1,0:T(8,128)(2,1)S(1)} collective-permute-done((bf16[128,1024]{1,0:T(8,128)(2,1)S(1)}, bf16[128,1024]{1,0:T(8,128)(2,1)S(1)}, u32[]{:S(2)}, u32[]{:S(2)}) %collective-permute-start) | collective-permute-done | bytes 262176 | tf_op jit(solution)/shard_map/ppermute | solution.py:24
  57.4 8.3 %collective-permute-done.7 = bf16[128,1024]{1,0:T(8,128)(2,1)S(1)} collective-permute-done((bf16[128,1024]{1,0:T(8,128)(2,1)S(1)}, bf16[128,1024]{1,0:T(8,128)(2,1)S(1)}, u32[]{:S(2)}, u32[]{:S(2)}) %collective-permute-start.7) | collective-permute-done | bytes 262176 | tf_op jit(solution)/shard_map/ppermute | solution.py:24
  69.6 5.4 %collective-permute-start.13 = (bf16[2,80,1024]{2,1,0:T(8,128)(2,1)S(1)}, bf16[2,80,1024]{2,1,0:T(8,128)(2,1)S(1)}, u32[]{:S(2)}, u32[]{:S(2)}) collective-permute-start(bf16[2,80,1024]{2,1,0:T(8,128)(2,1)S(1)} %convert_element_type.219), channel_id=1, source_target_pairs={{0,1},{4,5},{8,9},{12,13},{16,17},{20,21},{24,25},{28,29}} | collective-permute-start | bytes 983048 | tf_op jit(solution)/shard_map/ppermute | solution.py:24
  75.7 5.4 %collective-permute-done.11 = bf16[4,80,1024]{2,1,0:T(8,128)(2,1)S(1)} collective-permute-done((bf16[4,80,1024]{2,1,0:T(8,128)(2,1)S(1)}, bf16[4,80,1024]{2,1,0:T(8,128)(2,1)S(1)}, u32[]{:S(2)}, u32[]{:S(2)}) %collective-permute-start.11) | collective-permute-done | bytes 655392 | tf_op jit(solution)/shard_map/ppermute | solution.py:24
  82.1 6.1 %collective-permute-start.17 = (bf16[2,80,1024]{2,1,0:T(8,128)(2,1)S(1)}, bf16[2,80,1024]{2,1,0:T(8,128)(2,1)S(1)}, u32[]{:S(2)}, u32[]{:S(2)}) collective-permute-start(bf16[2,80,1024]{2,1,0:T(8,128)(2,1)S(1)} %get-tuple-element.147), channel_id=1, source_target_pairs={{0,1},{1,2},{4,5},{5,6},{8,9},{9,10},{12,13},{13,14},{16,17},{17,1... | collective-permute-start | bytes 983048 | tf_op jit(solution)/shard_map/ppermute | solution.py:24
  91.1 2.9 %fusion.2 = f32[640,2048]{1,0:T(8,128)S(1)} fusion(bf16[640,1024]{1,0:T(8,128)(2,1)S(1)} %bitcast.208, bf16[1,1,1024,2048]{3,2,1,0:T(8,128)(2,1)S(1)} %copy-done.9), kind=kOutput, calls=%fused_computation.2 | convolution fusion | flops 2684354560 | bytes 10747904 | tf_op jit(solution)/shard_map/dot_general | solution.py:207
  96.8 4.3 %collective-permute-start.19 = (bf16[2,80,1024]{2,1,0:T(8,128)(2,1)S(1)}, bf16[2,80,1024]{2,1,0:T(8,128)(2,1)S(1)}, u32[]{:S(2)}, u32[]{:S(2)}) collective-permute-start(bf16[2,80,1024]{2,1,0:T(8,128)(2,1)S(1)} %add_convert_fusion.7), channel_id=1, source_target_pairs={{0,1},{1,2},{2,3},{4,5},{5,6},{6,7},{8,9},{9,10},{10,11},{12,13},{... | collective-permute-start | bytes 983048 | tf_op jit(solution)/shard_map/ppermute | solution.py:24
  102.4 4.6 %collective-permute-start.15 = (bf16[2,80,2048]{2,1,0:T(8,128)(2,1)S(1)}, bf16[2,80,2048]{2,1,0:T(8,128)(2,1)S(1)}, u32[]{:S(2)}, u32[]{:S(2)}) collective-permute-start(bf16[2,80,2048]{2,1,0:T(8,128)(2,1)S(1)} %convert_element_type.225), channel_id=1, source_target_pairs={{0,1},{4,5},{8,9},{12,13},{16,17},{20,21},{24,25},{28,29}} | collective-permute-start | bytes 1966088 | tf_op jit(solution)/shard_map/ppermute | solution.py:24
  112.2 4.2 %collective-permute-start.23 = (bf16[2,80,2048]{2,1,0:T(8,128)(2,1)}, bf16[2,80,2048]{2,1,0:T(8,128)(2,1)}, u32[]{:S(2)}, u32[]{:S(2)}) collective-permute-start(bf16[2,80,2048]{2,1,0:T(8,128)(2,1)} %pad_maximum_fusion.6), channel_id=1, source_target_pairs={{0,1},{1,2},{2,3},{4,5},{5,6},{6,7},{8,9},{9,10},{10,11},{12,13},{... | collective-permute-start | bytes 1966088 | tf_op jit(solution)/shard_map/ppermute | solution.py:24
  117.7 4.4 %collective-permute-done.15 = bf16[2,80,2048]{2,1,0:T(8,128)(2,1)S(1)} collective-permute-done((bf16[2,80,2048]{2,1,0:T(8,128)(2,1)S(1)}, bf16[2,80,2048]{2,1,0:T(8,128)(2,1)S(1)}, u32[]{:S(2)}, u32[]{:S(2)}) %collective-permute-start.15) | collective-permute-done | bytes 655392 | tf_op jit(solution)/shard_map/ppermute | solution.py:24
  123.5 5.2 %collective-permute-start.21 = (bf16[2,80,2048]{2,1,0:T(8,128)(2,1)}, bf16[2,80,2048]{2,1,0:T(8,128)(2,1)}, u32[]{:S(2)}, u32[]{:S(2)}) collective-permute-start(bf16[2,80,2048]{2,1,0:T(8,128)(2,1)} %get-tuple-element.141), channel_id=1, source_target_pairs={{0,1},{1,2},{4,5},{5,6},{8,9},{9,10},{12,13},{13,14},{16,17},{17,1... | collective-permute-start | bytes 1966088 | tf_op jit(solution)/shard_map/ppermute | solution.py:24
  131.5 4.7 %collective-permute-done.23 = bf16[2,80,2048]{2,1,0:T(8,128)(2,1)} collective-permute-done((bf16[2,80,2048]{2,1,0:T(8,128)(2,1)}, bf16[2,80,2048]{2,1,0:T(8,128)(2,1)}, u32[]{:S(2)}, u32[]{:S(2)}) %collective-permute-start.23) | collective-permute-done | bytes 655392 | tf_op jit(solution)/shard_map/ppermute | solution.py:24
  139.1 9.6 %collective-permute-done.21 = bf16[2,80,2048]{2,1,0:T(8,128)(2,1)} collective-permute-done((bf16[2,80,2048]{2,1,0:T(8,128)(2,1)}, bf16[2,80,2048]{2,1,0:T(8,128)(2,1)}, u32[]{:S(2)}, u32[]{:S(2)}) %collective-permute-start.21) | collective-permute-done | bytes 655392 | tf_op jit(solution)/shard_map/ppermute | solution.py:24
  154.6 5.1 %collective-permute-start.25 = (bf16[2,80,2048]{2,1,0:T(8,128)(2,1)}, bf16[2,80,2048]{2,1,0:T(8,128)(2,1)S(1)}, u32[]{:S(2)}, u32[]{:S(2)}) collective-permute-start(bf16[2,80,2048]{2,1,0:T(8,128)(2,1)} %add_convert_fusion.3), channel_id=1, source_target_pairs={{0,1},{1,2},{2,3},{4,5},{5,6},{6,7},{8,9},{9,10},{10,11},{12,13},{... | collective-permute-start | bytes 1966088 | tf_op jit(solution)/shard_map/ppermute | solution.py:24
  163.5 10.0 %collective-permute-done.26 = bf16[2,80,2048]{2,1,0:T(8,128)(2,1)S(1)} collective-permute-done((bf16[2,80,2048]{2,1,0:T(8,128)(2,1)}, bf16[2,80,2048]{2,1,0:T(8,128)(2,1)S(1)}, u32[]{:S(2)}, u32[]{:S(2)}) %collective-permute-start.26) | collective-permute-done | bytes 655392 | tf_op jit(solution)/shard_map/ppermute | solution.py:24
  175.3 4.0 %collective-permute-start.29 = (bf16[2,80,1024]{2,1,0:T(8,128)(2,1)S(1)}, bf16[2,80,1024]{2,1,0:T(8,128)(2,1)S(1)}, u32[]{:S(2)}, u32[]{:S(2)}) collective-permute-start(bf16[2,80,1024]{2,1,0:T(8,128)(2,1)S(1)} %fusion.26), channel_id=1, source_target_pairs={{0,1},{1,2},{2,3},{4,5},{5,6},{6,7},{8,9},{9,10},{10,11},{12,13},{... | collective-permute-start | bytes 983048 | tf_op jit(solution)/shard_map/ppermute | solution.py:24
  181.8 5.7 %collective-permute-done.32 = bf16[2,80,2048]{2,1,0:T(8,128)(2,1)S(1)} collective-permute-done((bf16[2,80,2048]{2,1,0:T(8,128)(2,1)}, bf16[2,80,2048]{2,1,0:T(8,128)(2,1)S(1)}, u32[]{:S(2)}, u32[]{:S(2)}) %collective-permute-start.32) | collective-permute-done | bytes 655392 | tf_op jit(solution)/shard_map/ppermute | solution.py:24
  191.1 2.9 %fusion.8 = bf16[640,1024]{1,0:T(8,128)(2,1)S(1)} fusion(bf16[640,2048]{1,0:T(8,128)(2,1)S(1)} %bitcast.202, bf16[1,1,1024,2048]{3,2,1,0:T(8,128)(2,1)S(1)} %copy-done.10), kind=kOutput, calls=%fused_computation.13 | convolution fusion | flops 2685009920 | bytes 8126464 | tf_op jit(solution)/shard_map/dot_general | solution.py:54
  196.1 4.6 %collective-permute-start.48 = (bf16[80,1024]{1,0:T(8,128)(2,1)S(1)}, bf16[80,1024]{1,0:T(8,128)(2,1)S(1)}, u32[]{:S(2)}, u32[]{:S(2)}) collective-permute-start(bf16[80,1024]{1,0:T(8,128)(2,1)S(1)} %get-tuple-element.101), channel_id=1, source_target_pairs={{0,29},{1,30},{2,31},{3,28},{4,25},{5,26},{6,27},{7,24},{8,5},{9,6... | collective-permute-start | bytes 491528 | tf_op jit(solution)/shard_map/ppermute | solution.py:24
  201.5 8.1 %collective-permute-start.50 = (bf16[80,1024]{1,0:T(8,128)(2,1)S(1)}, bf16[80,1024]{1,0:T(8,128)(2,1)S(1)}, u32[]{:S(2)}, u32[]{:S(2)}) collective-permute-start(bf16[80,1024]{1,0:T(8,128)(2,1)S(1)} %get-tuple-element.103), channel_id=1, source_target_pairs={{0,31},{1,28},{2,29},{3,30},{4,27},{5,24},{6,25},{7,26},{8,7},{9,4... | collective-permute-start | bytes 491528 | tf_op jit(solution)/shard_map/ppermute | solution.py:24
  210.3 3.2 %collective-permute-done.34 = bf16[2,80,1024]{2,1,0:T(8,128)(2,1)S(1)} collective-permute-done((bf16[2,80,1024]{2,1,0:T(8,128)(2,1)S(1)}, bf16[2,80,1024]{2,1,0:T(8,128)(2,1)S(1)}, u32[]{:S(2)}, u32[]{:S(2)}) %collective-permute-start.34) | collective-permute-done | bytes 327712 | tf_op jit(solution)/shard_map/ppermute | solution.py:24
  213.6 11.5 %collective-permute-start.47 = (bf16[80,1024]{1,0:T(8,128)(2,1)S(1)}, bf16[80,1024]{1,0:T(8,128)(2,1)S(1)}, u32[]{:S(2)}, u32[]{:S(2)}) collective-permute-start(bf16[80,1024]{1,0:T(8,128)(2,1)S(1)} %get-tuple-element.129), channel_id=1, source_target_pairs={{0,25},{1,26},{2,27},{3,24},{4,29},{5,30},{6,31},{7,28},{8,1},{9,2... | collective-permute-start | bytes 491528 | tf_op jit(solution)/shard_map/ppermute | solution.py:24
  227.3 5.9 %collective-permute-done.46 = bf16[80,1024]{1,0:T(8,128)(2,1)S(1)} collective-permute-done((bf16[80,1024]{1,0:T(8,128)(2,1)S(1)}, bf16[80,1024]{1,0:T(8,128)(2,1)S(1)}, u32[]{:S(2)}, u32[]{:S(2)}) %collective-permute-start.46) | collective-permute-done | bytes 163872 | tf_op jit(solution)/shard_map/ppermute | solution.py:24
  235.6 6.5 %collective-permute-done.36 = bf16[2,80,1024]{2,1,0:T(8,128)(2,1)S(1)} collective-permute-done((bf16[2,80,1024]{2,1,0:T(8,128)(2,1)S(1)}, bf16[2,80,1024]{2,1,0:T(8,128)(2,1)S(1)}, u32[]{:S(2)}, u32[]{:S(2)}) %collective-permute-start.36) | collective-permute-done | bytes 327712 | tf_op jit(solution)/shard_map/ppermute | solution.py:24
  244.1 5.6 %collective-permute-start.38 = (bf16[80,1024]{1,0:T(8,128)(2,1)S(1)}, bf16[80,1024]{1,0:T(8,128)(2,1)S(1)}, u32[]{:S(2)}, u32[]{:S(2)}) collective-permute-start(bf16[80,1024]{1,0:T(8,128)(2,1)S(1)} %get-tuple-element.138), channel_id=1, source_target_pairs={{0,14},{1,15},{2,12},{3,13},{4,10},{5,11},{6,8},{7,9},{8,22},{9,23... | collective-permute-start | bytes 491528 | tf_op jit(solution)/shard_map/ppermute | solution.py:24
  255.2 11.1 %collective-permute-done.37 = bf16[80,1024]{1,0:T(8,128)(2,1)S(1)} collective-permute-done((bf16[80,1024]{1,0:T(8,128)(2,1)S(1)}, bf16[80,1024]{1,0:T(8,128)(2,1)S(1)}, u32[]{:S(2)}, u32[]{:S(2)}) %collective-permute-start.37) | collective-permute-done | bytes 163872 | tf_op jit(solution)/shard_map/ppermute | solution.py:24
  266.3 3.7 %collective-permute-done.38 = bf16[80,1024]{1,0:T(8,128)(2,1)S(1)} collective-permute-done((bf16[80,1024]{1,0:T(8,128)(2,1)S(1)}, bf16[80,1024]{1,0:T(8,128)(2,1)S(1)}, u32[]{:S(2)}, u32[]{:S(2)}) %collective-permute-start.38) | collective-permute-done | bytes 163872 | tf_op jit(solution)/shard_map/ppermute | solution.py:24
  277.0 2.9 %collective-permute-done.44 = bf16[80,1024]{1,0:T(8,128)(2,1)S(1)} collective-permute-done((bf16[80,1024]{1,0:T(8,128)(2,1)S(1)}, bf16[80,1024]{1,0:T(8,128)(2,1)S(1)}, u32[]{:S(2)}, u32[]{:S(2)}) %collective-permute-start.44) | collective-permute-done | bytes 163872 | tf_op jit(solution)/shard_map/ppermute | solution.py:24
  (171 shorter events, 94.3 us)
Async XLA Ops:
  5.4 30.1 %collective-permute-start.1 = (bf16[128,1024]{1,0:T(8,128)(2,1)S(1)}, bf16[128,1024]{1,0:T(8,128)(2,1)}, u32[]{:S(2)}, u32[]{:S(2)}) collective-permute-start(bf16[128,1024]{1,0:T(8,128)(2,1)S(1)} %convolution_convert_fusion.5), channel_id=1, source_target_pairs={{0,2},{1,3},{2,0},{3,1},{4,6},{5,7},{6,4},{7,5},{8,10},{9,11},{10,... | collective-permute-start | bytes 786440 | tf_op jit(solution)/shard_map/ppermute | solution.py:24
  10.4 27.8 %collective-permute-start.2 = (bf16[128,1024]{1,0:T(8,128)(2,1)}, bf16[128,1024]{1,0:T(8,128)(2,1)}, u32[]{:S(2)}, u32[]{:S(2)}) collective-permute-start(bf16[128,1024]{1,0:T(8,128)(2,1)} %convolution_convert_fusion.4), channel_id=1, source_target_pairs={{0,3},{1,0},{2,1},{3,2},{4,7},{5,4},{6,5},{7,6},{8,11},{9,8},{10,9... | collective-permute-start | bytes 786440 | tf_op jit(solution)/shard_map/ppermute | solution.py:24
  11.7 34.5 %collective-permute-start.4 = (bf16[128,4096]{1,0:T(8,128)(2,1)}, bf16[128,4096]{1,0:T(8,128)(2,1)}, u32[]{:S(2)}, u32[]{:S(2)}) collective-permute-start(bf16[128,4096]{1,0:T(8,128)(2,1)} %bitcast.209), channel_id=1, source_target_pairs={{0,24},{1,25},{2,26},{3,27},{4,28},{5,29},{6,30},{7,31},{8,0},{9,1... | collective-permute-start | bytes 3145736 | tf_op jit(solution)/shard_map/ppermute | solution.py:24
  12.1 22.7 %collective-permute-start.5 = (s32[128]{0:T(128)S(1)}, s32[128]{0:T(128)S(1)}, u32[]{:S(2)}, u32[]{:S(2)}) collective-permute-start(s32[128]{0:T(128)S(1)} %bitcast.219), channel_id=1, source_target_pairs={{0,24},{1,25},{2,26},{3,27},{4,28},{5,29},{6,30},{7,31},{8,0},{9,1... | collective-permute-start | bytes 1544 | tf_op jit(solution)/shard_map/ppermute | solution.py:24
  13.4 44.0 %collective-permute-start.9 = (bf16[128,4096]{1,0:T(8,128)(2,1)}, bf16[128,4096]{1,0:T(8,128)(2,1)}, u32[]{:S(2)}, u32[]{:S(2)}) collective-permute-start(bf16[128,4096]{1,0:T(8,128)(2,1)} %bitcast.210), channel_id=1, source_target_pairs={{0,8},{1,9},{2,10},{3,11},{4,12},{5,13},{6,14},{7,15},{8,16},{9,17... | collective-permute-start | bytes 3145736 | tf_op jit(solution)/shard_map/ppermute | solution.py:24
  38.2 19.2 %collective-permute-start = (bf16[128,1024]{1,0:T(8,128)(2,1)S(1)}, bf16[128,1024]{1,0:T(8,128)(2,1)S(1)}, u32[]{:S(2)}, u32[]{:S(2)}) collective-permute-start(bf16[128,1024]{1,0:T(8,128)(2,1)S(1)} %convolution_convert_fusion.8), channel_id=1, source_target_pairs={{0,2},{1,3},{2,0},{3,1},{4,6},{5,7},{6,4},{7,5},{8,10},{9,11},{10,... | collective-permute-start | bytes 786440 | tf_op jit(solution)/shard_map/ppermute | solution.py:24
  46.2 19.4 %collective-permute-start.7 = (bf16[128,1024]{1,0:T(8,128)(2,1)S(1)}, bf16[128,1024]{1,0:T(8,128)(2,1)S(1)}, u32[]{:S(2)}, u32[]{:S(2)}) collective-permute-start(bf16[128,1024]{1,0:T(8,128)(2,1)S(1)} %copy-done.7), channel_id=1, source_target_pairs={{0,3},{1,0},{2,1},{3,2},{4,7},{5,4},{6,5},{7,6},{8,11},{9,8},{10,9... | collective-permute-start | bytes 786440 | tf_op jit(solution)/shard_map/ppermute | solution.py:24
  50.5 16.9 %collective-permute-start.12 = (bf16[4,80,1024]{2,1,0:T(8,128)(2,1)S(1)}, bf16[4,80,1024]{2,1,0:T(8,128)(2,1)S(1)}, u32[]{:S(2)}, u32[]{:S(2)}) collective-permute-start(bf16[4,80,1024]{2,1,0:T(8,128)(2,1)S(1)} %get-tuple-element.145), channel_id=1, source_target_pairs={{0,4},{1,5},{2,6},{3,7},{4,0},{5,1},{6,2},{7,3},{8,12},{9,13},{10,... | collective-permute-start | bytes 1966088 | tf_op jit(solution)/shard_map/ppermute | solution.py:24
  102.4 19.7 %collective-permute-start.15 = (bf16[2,80,2048]{2,1,0:T(8,128)(2,1)S(1)}, bf16[2,80,2048]{2,1,0:T(8,128)(2,1)S(1)}, u32[]{:S(2)}, u32[]{:S(2)}) collective-permute-start(bf16[2,80,2048]{2,1,0:T(8,128)(2,1)S(1)} %convert_element_type.225), channel_id=1, source_target_pairs={{0,1},{4,5},{8,9},{12,13},{16,17},{20,21},{24,25},{28,29}} | collective-permute-start | bytes 1966088 | tf_op jit(solution)/shard_map/ppermute | solution.py:24
  112.2 24.1 %collective-permute-start.23 = (bf16[2,80,2048]{2,1,0:T(8,128)(2,1)}, bf16[2,80,2048]{2,1,0:T(8,128)(2,1)}, u32[]{:S(2)}, u32[]{:S(2)}) collective-permute-start(bf16[2,80,2048]{2,1,0:T(8,128)(2,1)} %pad_maximum_fusion.6), channel_id=1, source_target_pairs={{0,1},{1,2},{2,3},{4,5},{5,6},{6,7},{8,9},{9,10},{10,11},{12,13},{... | collective-permute-start | bytes 1966088 | tf_op jit(solution)/shard_map/ppermute | solution.py:24
  116.4 19.9 %collective-permute-start.24 = (bf16[2,80,2048]{2,1,0:T(8,128)(2,1)}, bf16[2,80,2048]{2,1,0:T(8,128)(2,1)}, u32[]{:S(2)}, u32[]{:S(2)}) collective-permute-start(bf16[2,80,2048]{2,1,0:T(8,128)(2,1)} %pad_maximum_fusion.6), channel_id=1, source_target_pairs={{1,0},{2,1},{3,2},{5,4},{6,5},{7,6},{9,8},{10,9},{11,10},{13,12},{... | collective-permute-start | bytes 1966088 | tf_op jit(solution)/shard_map/ppermute | solution.py:24
  123.5 25.2 %collective-permute-start.21 = (bf16[2,80,2048]{2,1,0:T(8,128)(2,1)}, bf16[2,80,2048]{2,1,0:T(8,128)(2,1)}, u32[]{:S(2)}, u32[]{:S(2)}) collective-permute-start(bf16[2,80,2048]{2,1,0:T(8,128)(2,1)} %get-tuple-element.141), channel_id=1, source_target_pairs={{0,1},{1,2},{4,5},{5,6},{8,9},{9,10},{12,13},{13,14},{16,17},{17,1... | collective-permute-start | bytes 1966088 | tf_op jit(solution)/shard_map/ppermute | solution.py:24
  128.8 20.0 %collective-permute-start.22 = (bf16[2,80,2048]{2,1,0:T(8,128)(2,1)}, bf16[2,80,2048]{2,1,0:T(8,128)(2,1)}, u32[]{:S(2)}, u32[]{:S(2)}) collective-permute-start(bf16[2,80,2048]{2,1,0:T(8,128)(2,1)} %get-tuple-element.140), channel_id=1, source_target_pairs={{2,1},{3,2},{6,5},{7,6},{10,9},{11,10},{14,13},{15,14},{18,17},{19... | collective-permute-start | bytes 1966088 | tf_op jit(solution)/shard_map/ppermute | solution.py:24
  136.3 25.1 %collective-permute-start.27 = (bf16[2,80,2048]{2,1,0:T(8,128)(2,1)}, bf16[2,80,2048]{2,1,0:T(8,128)(2,1)}, u32[]{:S(2)}, u32[]{:S(2)}) collective-permute-start(bf16[2,80,2048]{2,1,0:T(8,128)(2,1)} %collective-permute-done.23), channel_id=1, source_target_pairs={{1,2},{2,3},{5,6},{6,7},{9,10},{10,11},{13,14},{14,15},{17,18},{18... | collective-permute-start | bytes 1966088 | tf_op jit(solution)/shard_map/ppermute | solution.py:24
  137.8 23.5 %collective-permute-start.28 = (bf16[2,80,2048]{2,1,0:T(8,128)(2,1)}, bf16[2,80,2048]{2,1,0:T(8,128)(2,1)}, u32[]{:S(2)}, u32[]{:S(2)}) collective-permute-start(bf16[2,80,2048]{2,1,0:T(8,128)(2,1)} %collective-permute-done.24), channel_id=1, source_target_pairs={{1,0},{2,1},{5,4},{6,5},{9,8},{10,9},{13,12},{14,13},{17,16},{18,1... | collective-permute-start | bytes 1966088 | tf_op jit(solution)/shard_map/ppermute | solution.py:24
  153.3 20.2 %collective-permute-start.26 = (bf16[2,80,2048]{2,1,0:T(8,128)(2,1)}, bf16[2,80,2048]{2,1,0:T(8,128)(2,1)S(1)}, u32[]{:S(2)}, u32[]{:S(2)}) collective-permute-start(bf16[2,80,2048]{2,1,0:T(8,128)(2,1)} %add_convert_fusion.2), channel_id=1, source_target_pairs={{1,0},{2,1},{3,2},{5,4},{6,5},{7,6},{9,8},{10,9},{11,10},{13,12},{... | collective-permute-start | bytes 1966088 | tf_op jit(solution)/shard_map/ppermute | solution.py:24
  154.6 18.9 %collective-permute-start.25 = (bf16[2,80,2048]{2,1,0:T(8,128)(2,1)}, bf16[2,80,2048]{2,1,0:T(8,128)(2,1)S(1)}, u32[]{:S(2)}, u32[]{:S(2)}) collective-permute-start(bf16[2,80,2048]{2,1,0:T(8,128)(2,1)} %add_convert_fusion.3), channel_id=1, source_target_pairs={{0,1},{1,2},{2,3},{4,5},{5,6},{6,7},{8,9},{9,10},{10,11},{12,13},{... | collective-permute-start | bytes 1966088 | tf_op jit(solution)/shard_map/ppermute | solution.py:24
  161.4 20.5 %collective-permute-start.31 = (bf16[2,80,2048]{2,1,0:T(8,128)(2,1)}, bf16[2,80,2048]{2,1,0:T(8,128)(2,1)S(1)}, u32[]{:S(2)}, u32[]{:S(2)}) collective-permute-start(bf16[2,80,2048]{2,1,0:T(8,128)(2,1)} %collective-permute-done.27), channel_id=1, source_target_pairs={{2,3},{6,7},{10,11},{14,15},{18,19},{22,23},{26,27},{30,31}} | collective-permute-start | bytes 1966088 | tf_op jit(solution)/shard_map/ppermute | solution.py:24
  162.2 25.3 %collective-permute-start.32 = (bf16[2,80,2048]{2,1,0:T(8,128)(2,1)}, bf16[2,80,2048]{2,1,0:T(8,128)(2,1)S(1)}, u32[]{:S(2)}, u32[]{:S(2)}) collective-permute-start(bf16[2,80,2048]{2,1,0:T(8,128)(2,1)} %collective-permute-done.28), channel_id=1, source_target_pairs={{1,0},{5,4},{9,8},{13,12},{17,16},{21,20},{25,24},{29,28}} | collective-permute-start | bytes 1966088 | tf_op jit(solution)/shard_map/ppermute | solution.py:24
  175.3 18.7 %collective-permute-start.29 = (bf16[2,80,1024]{2,1,0:T(8,128)(2,1)S(1)}, bf16[2,80,1024]{2,1,0:T(8,128)(2,1)S(1)}, u32[]{:S(2)}, u32[]{:S(2)}) collective-permute-start(bf16[2,80,1024]{2,1,0:T(8,128)(2,1)S(1)} %fusion.26), channel_id=1, source_target_pairs={{0,1},{1,2},{2,3},{4,5},{5,6},{6,7},{8,9},{9,10},{10,11},{12,13},{... | collective-permute-start | bytes 983048 | tf_op jit(solution)/shard_map/ppermute | solution.py:24
  194.7 18.9 %collective-permute-start.34 = (bf16[2,80,1024]{2,1,0:T(8,128)(2,1)S(1)}, bf16[2,80,1024]{2,1,0:T(8,128)(2,1)S(1)}, u32[]{:S(2)}, u32[]{:S(2)}) collective-permute-start(bf16[2,80,1024]{2,1,0:T(8,128)(2,1)S(1)} %collective-permute-done.30), channel_id=1, source_target_pairs={{1,0},{2,1},{5,4},{6,5},{9,8},{10,9},{13,12},{14,13},{17,16},{18,1... | collective-permute-start | bytes 983048 | tf_op jit(solution)/shard_map/ppermute | solution.py:24
  196.1 17.5 %collective-permute-start.48 = (bf16[80,1024]{1,0:T(8,128)(2,1)S(1)}, bf16[80,1024]{1,0:T(8,128)(2,1)S(1)}, u32[]{:S(2)}, u32[]{:S(2)}) collective-permute-start(bf16[80,1024]{1,0:T(8,128)(2,1)S(1)} %get-tuple-element.101), channel_id=1, source_target_pairs={{0,29},{1,30},{2,31},{3,28},{4,25},{5,26},{6,27},{7,24},{8,5},{9,6... | collective-permute-start | bytes 491528 | tf_op jit(solution)/shard_map/ppermute | solution.py:24
  200.7 24.4 %collective-permute-start.49 = (bf16[80,1024]{1,0:T(8,128)(2,1)S(1)}, bf16[80,1024]{1,0:T(8,128)(2,1)S(1)}, u32[]{:S(2)}, u32[]{:S(2)}) collective-permute-start(bf16[80,1024]{1,0:T(8,128)(2,1)S(1)} %get-tuple-element.102), channel_id=1, source_target_pairs={{0,27},{1,24},{2,25},{3,26},{4,31},{5,28},{6,29},{7,30},{8,3},{9,0... | collective-permute-start | bytes 491528 | tf_op jit(solution)/shard_map/ppermute | solution.py:24
  201.5 25.1 %collective-permute-start.50 = (bf16[80,1024]{1,0:T(8,128)(2,1)S(1)}, bf16[80,1024]{1,0:T(8,128)(2,1)S(1)}, u32[]{:S(2)}, u32[]{:S(2)}) collective-permute-start(bf16[80,1024]{1,0:T(8,128)(2,1)S(1)} %get-tuple-element.103), channel_id=1, source_target_pairs={{0,31},{1,28},{2,29},{3,30},{4,27},{5,24},{6,25},{7,26},{8,7},{9,4... | collective-permute-start | bytes 491528 | tf_op jit(solution)/shard_map/ppermute | solution.py:24
  209.8 16.8 %collective-permute-start.45 = (bf16[80,1024]{1,0:T(8,128)(2,1)S(1)}, bf16[80,1024]{1,0:T(8,128)(2,1)S(1)}, u32[]{:S(2)}, u32[]{:S(2)}) collective-permute-start(bf16[80,1024]{1,0:T(8,128)(2,1)S(1)} %get-tuple-element.131), channel_id=1, source_target_pairs={{0,26},{1,27},{2,24},{3,25},{4,30},{5,31},{6,28},{7,29},{8,2},{9,3... | collective-permute-start | bytes 491528 | tf_op jit(solution)/shard_map/ppermute | solution.py:24
  213.6 19.7 %collective-permute-start.46 = (bf16[80,1024]{1,0:T(8,128)(2,1)S(1)}, bf16[80,1024]{1,0:T(8,128)(2,1)S(1)}, u32[]{:S(2)}, u32[]{:S(2)}) collective-permute-start(bf16[80,1024]{1,0:T(8,128)(2,1)S(1)} %get-tuple-element.130), channel_id=1, source_target_pairs={{0,30},{1,31},{2,28},{3,29},{4,26},{5,27},{6,24},{7,25},{8,6},{9,7... | collective-permute-start | bytes 491528 | tf_op jit(solution)/shard_map/ppermute | solution.py:24
  213.6 20.9 %collective-permute-start.47 = (bf16[80,1024]{1,0:T(8,128)(2,1)S(1)}, bf16[80,1024]{1,0:T(8,128)(2,1)S(1)}, u32[]{:S(2)}, u32[]{:S(2)}) collective-permute-start(bf16[80,1024]{1,0:T(8,128)(2,1)S(1)} %get-tuple-element.129), channel_id=1, source_target_pairs={{0,25},{1,26},{2,27},{3,24},{4,29},{5,30},{6,31},{7,28},{8,1},{9,2... | collective-permute-start | bytes 491528 | tf_op jit(solution)/shard_map/ppermute | solution.py:24
  244.1 22.2 %collective-permute-start.37 = (bf16[80,1024]{1,0:T(8,128)(2,1)S(1)}, bf16[80,1024]{1,0:T(8,128)(2,1)S(1)}, u32[]{:S(2)}, u32[]{:S(2)}) collective-permute-start(bf16[80,1024]{1,0:T(8,128)(2,1)S(1)} %get-tuple-element.139), channel_id=1, source_target_pairs={{0,10},{1,11},{2,8},{3,9},{4,14},{5,15},{6,12},{7,13},{8,18},{9,19... | collective-permute-start | bytes 491528 | tf_op jit(solution)/shard_map/ppermute | solution.py:24
  244.1 25.8 %collective-permute-start.38 = (bf16[80,1024]{1,0:T(8,128)(2,1)S(1)}, bf16[80,1024]{1,0:T(8,128)(2,1)S(1)}, u32[]{:S(2)}, u32[]{:S(2)}) collective-permute-start(bf16[80,1024]{1,0:T(8,128)(2,1)S(1)} %get-tuple-element.138), channel_id=1, source_target_pairs={{0,14},{1,15},{2,12},{3,13},{4,10},{5,11},{6,8},{7,9},{8,22},{9,23... | collective-permute-start | bytes 491528 | tf_op jit(solution)/shard_map/ppermute | solution.py:24
  249.7 21.2 %collective-permute-start.39 = (bf16[80,1024]{1,0:T(8,128)(2,1)S(1)}, bf16[80,1024]{1,0:T(8,128)(2,1)S(1)}, u32[]{:S(2)}, u32[]{:S(2)}) collective-permute-start(bf16[80,1024]{1,0:T(8,128)(2,1)S(1)} %get-tuple-element.137), channel_id=1, source_target_pairs={{0,9},{1,10},{2,11},{3,8},{4,13},{5,14},{6,15},{7,12},{8,17},{9,18... | collective-permute-start | bytes 491528 | tf_op jit(solution)/shard_map/ppermute | solution.py:24
  251.4 23.5 %collective-permute-start.40 = (bf16[80,1024]{1,0:T(8,128)(2,1)S(1)}, bf16[80,1024]{1,0:T(8,128)(2,1)S(1)}, u32[]{:S(2)}, u32[]{:S(2)}) collective-permute-start(bf16[80,1024]{1,0:T(8,128)(2,1)S(1)} %get-tuple-element.136), channel_id=1, source_target_pairs={{0,13},{1,14},{2,15},{3,12},{4,9},{5,10},{6,11},{7,8},{8,21},{9,22... | collective-permute-start | bytes 491528 | tf_op jit(solution)/shard_map/ppermute | solution.py:24
  252.6 22.4 %collective-permute-start.41 = (bf16[80,1024]{1,0:T(8,128)(2,1)S(1)}, bf16[80,1024]{1,0:T(8,128)(2,1)S(1)}, u32[]{:S(2)}, u32[]{:S(2)}) collective-permute-start(bf16[80,1024]{1,0:T(8,128)(2,1)S(1)} %get-tuple-element.135), channel_id=1, source_target_pairs={{0,11},{1,8},{2,9},{3,10},{4,15},{5,12},{6,13},{7,14},{8,19},{9,16... | collective-permute-start | bytes 491528 | tf_op jit(solution)/shard_map/ppermute | solution.py:24
  (34 other events, 438.0 us)
